TPU v7x, 512 devices: a whole 4x8x8 slice. The times are simulated.
512 devices in a mesh: row: 16 (over z_hi, y), col: 8 (over z_lo, core), depth: 4 (over x).
Axes of the slice: x: 4, y: 8, z: 8 (z_hi: 2, z_lo: 4; z = z_hi * 4 + z_lo), core: 2. Of those that a mesh axis runs over, the one named last changes fastest.
Arguments:
- features: float32 [65536, 128], P(('row', 'col', 'depth')), may hold values from -6 to 6
- weight: float32 [128, 128], replicated, may hold values from -0.5 to 0.5
- tile_values: bfloat16 [16, 8, 4, 16, 128, 128], P('row', 'col', 'depth'), may hold values from -2 to 2
- tile_index: int32 [16, 8, 4, 16], P('row', 'col', 'depth'), may hold values from 0 to 511, as said below
- tile_counts: int32 [16, 8, 4], P('row', 'col', 'depth'), may hold values from 4 to 16, as said below
- cotangent: float32 [65536, 128], P(('row', 'col', 'depth')), may hold values from -12 to 12
Outputs:
- output: float32 [65536, 128], P(('row', 'col', 'depth'))
- weight_grad: float32 [128, 128], replicated
- feature_grad: float32 [65536, 128], P(('row', 'col', 'depth'))
Inputs may be any that keep to these rules, and one draw needn't show every extreme that they name: `tile_index`: within one device the slot values are distinct; a value v places the tile at tile row v // 16 and tile column v % 16 of the device's block; only slots below tile_counts are live. `tile_counts`: some device has all 16 slots live.
All inputs are finite; a program needn't handle non-finite values.
Results may differ from a plain program's by a relative error of at most 0.0003.
Values sent between devices are 32-bit elements; how exact they have to be, the bound alone decides.
No kernel may reach another device: no remote copies, remote signals or barrier semaphores. Data moves between devices by JAX's collectives and lax.ppermute only.
A program may use at most 64 MiB of HBM per device.

v0:
```python
import math

import jax
import jax.numpy as jnp
from jax import lax
from jax.sharding import PartitionSpec as P


def select_table(block_pos, live_count, num_blocks):
    capacity = block_pos.shape[0]
    active = jnp.arange(capacity, dtype=jnp.int32) < live_count
    return (
        (block_pos[None, :] == jnp.arange(num_blocks, dtype=jnp.int32)[:, None]) & active[None, :]
    ).astype(jnp.float32)


def on_device(features, weight, tile_values, tile_index, tile_counts, cotangent):
    tile_data = tile_values.reshape(tile_values.shape[-3:]).astype(jnp.float32)
    slot_index = tile_index.reshape(-1)
    live_count = tile_counts.reshape(())
    capacity = tile_data.shape[0]
    tile_size = tile_data.shape[-1]
    piece_rows = features.shape[0]
    feat_width = features.shape[1]
    row_count = lax.axis_size("row")
    col_count = lax.axis_size("col")
    depth_count = lax.axis_size("depth")
    groups = col_count * depth_count
    row_blocks = groups * piece_rows // tile_size
    col_blocks = row_count * piece_rows // tile_size
    block_row = slot_index // col_blocks
    block_col = slot_index % col_blocks
    column_data = lax.all_gather(features, "row", axis=0, tiled=True)
    picked = column_data.reshape(col_blocks, tile_size, feat_width)[block_col]
    fwd_products = jnp.einsum(
        "tij,tjf->tif", tile_data, picked, precision=lax.Precision.HIGHEST
    ).reshape(capacity, tile_size * feat_width)
    fwd_table = select_table(block_row, live_count, row_blocks)
    table_part = fwd_table
    summed = jnp.dot(
        table_part,
        fwd_products,
        precision=lax.Precision.HIGHEST,
        preferred_element_type=jnp.float32,
    )
    aggregated = lax.psum_scatter(
        summed.reshape(lax.axis_size(("col", "depth")) * piece_rows, feat_width),
        ("col", "depth"),
        scatter_dimension=0,
        tiled=True,
    )
    pre_act = jnp.dot(
        aggregated, weight, precision=lax.Precision.HIGHEST, preferred_element_type=jnp.float32
    )
    sigma_pre = jax.nn.sigmoid(pre_act)
    output = pre_act * sigma_pre
    pre_grad = cotangent * sigma_pre * (1.0 + pre_act * (1.0 - sigma_pre))
    node_total = piece_rows * row_count * groups
    weight_term = jnp.dot(
        aggregated.T, pre_grad, precision=lax.Precision.HIGHEST, preferred_element_type=jnp.float32
    )
    weight_grad = lax.psum(weight_term, ("row", "col", "depth")) / math.sqrt(node_total)
    moving = jnp.dot(
        pre_grad, weight.T, precision=lax.Precision.HIGHEST, preferred_element_type=jnp.float32
    )
    slab_data = lax.all_gather(moving, ("col", "depth"), axis=0, tiled=True)
    back_picked = slab_data.reshape(row_blocks, tile_size, feat_width)[block_row]
    back_products = jnp.einsum(
        "tji,tjf->tif", tile_data, back_picked, precision=lax.Precision.HIGHEST
    ).reshape(capacity, tile_size * feat_width)
    back_table = select_table(block_col, live_count, col_blocks)
    table_part = back_table
    summed = jnp.dot(
        table_part,
        back_products,
        precision=lax.Precision.HIGHEST,
        preferred_element_type=jnp.float32,
    )
    summed_back = lax.psum_scatter(
        summed.reshape(lax.axis_size("row") * piece_rows, feat_width),
        "row",
        scatter_dimension=0,
        tiled=True,
    )
    return (output, weight_grad, summed_back)


def solution(mesh):
    return jax.shard_map(
        on_device,
        mesh=mesh,
        in_specs=(
            P(("row", "col", "depth"), None),
            P(),
            P("row", "col", "depth", None, None, None),
            P("row", "col", "depth", None),
            P("row", "col", "depth"),
            P(("row", "col", "depth"), None),
        ),
        out_specs=(P(("row", "col", "depth"), None), P(), P(("row", "col", "depth"), None)),
        check_vma=False,
    )
```

profile of v0, /device:TPU:2, one launch (start us, length us, event | category | flops | bytes accessed | tf_op | source)
XLA Modules:
  0.0 840.9 jit_solution(3113325342574788631)
XLA Ops:
  7.2 0.0 copy-start
  7.2 0.0 all-gather.3.cloned.1.call-start
  7.2 0.7 all-gather.3.cloned.1.call-update
  7.9 0.0 reduce-scatter.3.cloned.1.call-start
  8.6 0.7 fusion.18
  9.3 0.7 and_select_fusion.1
  10.0 99.3 %all-gather.3.cloned.1.call-done = f32[2048,128]{1,0:T(8,128)} async-done(((f32[128,128]{1,0:T(8,128)}), f32[2048,128]{1,0:T(8,128)}) %all-gather.3.cloned.1.call-update) | async-done | bytes 1048592 | tf_op jit(solution)/shard_map/all_gather | solution.py:33
  109.3 1.8 gather_fusion
  111.1 0.0 copy-done
  111.1 1.0 convolution_bitcast_fusion.1
  112.1 1.3 copy.10
  113.5 2.7 fusion.3
  116.1 1.5 reshape.214
  117.6 0.0 copy-start.1
  117.6 0.0 copy-start.2
  117.6 0.0 reduce-scatter.3.cloned.1.call-update
  117.7 0.0 all-gather.5.cloned.1.call-start
  117.7 139.9 %reduce-scatter.3.cloned.1.call-done = f32[128,128]{1,0:T(8,128)} async-done(((f32[4096,128]{1,0:T(8,128)}), f32[128,128]{1,0:T(8,128)}) %reduce-scatter.3.cloned.1.call-update) | async-done | bytes 65552 | tf_op jit(solution)/shard_map/reduce_scatter | solution.py:46
  257.6 0.0 copy-done.1
  257.6 1.7 fusion.8
  259.3 0.0 copy-done.2
  259.3 0.9 fusion.19
  260.2 0.0 all-gather.5.cloned.1.call-update
  260.3 0.0 all-reduce.2.cloned.1.call-start
  260.3 1.8 fusion.20
  262.1 0.0 all-reduce.2.cloned.1.call-update
  262.1 0.0 reduce-scatter.5.cloned.1.call-start
  262.2 87.3 %all-gather.5.cloned.1.call-done = f32[4096,128]{1,0:T(8,128)} async-done(((f32[128,128]{1,0:T(8,128)}), f32[4096,128]{1,0:T(8,128)}) %all-gather.5.cloned.1.call-update) | async-done | bytes 2097168 | tf_op jit(solution)/shard_map/all_gather | solution.py:66
  349.5 2.2 gather_fusion.1
  351.7 1.0 convolution_bitcast_fusion
  352.7 0.3 copy.12
  353.1 1.2 fusion
  354.3 1.1 reshape.217
  355.4 0.0 reduce-scatter.5.cloned.1.call-update
  355.4 255.8 %all-reduce.2.cloned.1.call-done = f32[128,128]{1,0:T(8,128)} async-done(((f32[128,128]{1,0:T(8,128)}), f32[128,128]{1,0:T(8,128)}) %all-reduce.2.cloned.1.call-update) | async-done | bytes 65552 | tf_op jit(solution)/shard_map/psum | solution.py:62
  611.2 1.5 broadcast_multiply_fusion
  612.7 221.7 %reduce-scatter.5.cloned.1.call-done = f32[128,128]{1,0:T(8,128)} async-done(((f32[2048,128]{1,0:T(8,128)}), f32[128,128]{1,0:T(8,128)}) %reduce-scatter.5.cloned.1.call-update) | async-done | bytes 65552 | tf_op jit(solution)/shard_map/reduce_scatter | solution.py:79
  (3 shorter events, 0.0 us)
Async XLA Ops:
  7.2 103.9 %copy-start = (bf16[1,1,1,16,128,128]{5,4,3,2,1,0:T(8,128)(2,1)S(1)}, bf16[1,1,1,16,128,128]{5,4,3,2,1,0:T(8,128)(2,1)}, u32[]{:S(2)}) copy-start(bf16[1,1,1,16,128,128]{5,4,3,2,1,0:T(8,128)(2,1)} %param.8) | copy-start | bytes 1572868
  7.2 102.1 %all-gather.3.cloned.1.call-start = ((), (), s32[]{:S(2)}) async-start(), calls=%async_computation.2 | async-start | bytes 1114112 | tf_op jit(solution)/shard_map/all_gather | solution.py:33
  7.9 249.7 %reduce-scatter.3.cloned.1.call-start = ((), (), s32[]{:S(2)}) async-start(), calls=%async_computation.3 | async-start | bytes 2162688 | tf_op jit(solution)/shard_map/reduce_scatter | solution.py:46
  117.6 140.0 %copy-start.1 = (f32[128,128]{1,0:T(8,128)S(1)}, f32[128,128]{1,0:T(8,128)}, u32[]{:S(2)}) copy-start(f32[128,128]{1,0:T(8,128)} %param.7) | copy-start | bytes 196612
  117.6 141.7 %copy-start.2 = (f32[128,128]{1,0:T(8,128)S(1)}, f32[128,128]{1,0:T(8,128)}, u32[]{:S(2)}) copy-start(f32[128,128]{1,0:T(8,128)} %param.11) | copy-start | bytes 196612
  117.7 231.8 %all-gather.5.cloned.1.call-start = ((), (), s32[]{:S(2)}) async-start(), calls=%async_computation.5 | async-start | bytes 2162688 | tf_op jit(solution)/shard_map/all_gather | solution.py:66
  260.3 350.9 %all-reduce.2.cloned.1.call-start = ((), (), s32[]{:S(2)}) async-start(), calls=%async_computation.4 | async-start | bytes 131072 | tf_op jit(solution)/shard_map/psum | solution.py:62
  262.1 572.3 %reduce-scatter.5.cloned.1.call-start = ((), (), s32[]{:S(2)}) async-start(), calls=%async_computation.6 | async-start | bytes 1114112 | tf_op jit(solution)/shard_map/reduce_scatter | solution.py:79
Sparse Core Ops, SparseCore 0:
  11.2 97.9 all-gather.2
  117.8 139.8 reduce-scatter.2
  260.5 88.9 all-gather.4
  355.7 255.4 all-reduce.1
  616.1 218.2 reduce-scatter.4
where the time goes:
time: 841 us
  waiting for transfers between devices  805 us (96%)
  between operations  14.5 us (2%)
  matrix products  10.3 us (1%)
    psum x1, waiting for transfers between devices, on_device(): lax.psum(weight_term, ('row', 'col', 'depth')) / math.sqrt(node_total)  256 us
    reduce_scatter x1, waiting for transfers between devices, on_device(): lax.psum_scatter(summed.reshape(lax.axis_size('row') * piece_rows, feat_w...  222 us
    reduce_scatter x1, waiting for transfers between devices, on_device(): lax.psum_scatter(summed.reshape(lax.axis_size(('col', 'depth')) * piece_r...  140 us
    all_gather x1, waiting for transfers between devices, on_device(): column_data = lax.all_gather(features, 'row', axis=0, tiled=True)  99.3 us
    all_gather x1, waiting for transfers between devices, on_device(): slab_data = lax.all_gather(moving, ('col', 'depth'), axis=0, tiled=True)  87.3 us
  transfers between devices with their start and end apart: 5, of which 5 were waited for; matrix products, arithmetic and copies ran while one was open for 1% of the time, Pallas kernels for 0%

commit v1 on v0

v1 whole, which is shorter than its diff:
```python
import functools
import math

import jax
import jax.numpy as jnp
from jax import lax
from jax.experimental import pallas as pl
from jax.experimental.pallas import tpu as pltpu
from jax.sharding import PartitionSpec as P

MEM = 48 * 1024 * 1024


def split_bf16(value):
    high = value.astype(jnp.bfloat16)
    low = (value - high.astype(jnp.float32)).astype(jnp.bfloat16)
    return high, low


def dot3(left, right, dims):
    lh, ll = split_bf16(left)
    rh, rl = split_bf16(right)

    def one(a, b):
        return lax.dot_general(a, b, (dims, ((), ())), preferred_element_type=jnp.float32)

    return one(lh, rh) + (one(lh, rl) + one(ll, rh))


def half_place(block, inner):
    return (block // inner) % 2, (block // (2 * inner)) * inner + block % inner


def forward_kernel(inner, index_ref, count_ref, tiles_ref, cols_ref, keep_ref, send_ref, acc, sems):
    capacity = tiles_ref.shape[0]
    col_blocks = cols_ref.shape[0]
    core = lax.axis_index("col") % 2
    acc[...] = jnp.zeros_like(acc)
    for slot in range(capacity):
        place = index_ref[slot]
        row, col = place // col_blocks, place % col_blocks
        half, spot = half_place(row, inner)
        data = jnp.where(slot < count_ref[0], cols_ref[col], 0.0)
        high, low = split_bf16(data)
        tile = tiles_ref[slot]
        product = jnp.dot(
            jnp.concatenate([tile, tile], axis=1),
            jnp.concatenate([high, low], axis=0),
            preferred_element_type=jnp.float32,
        )
        other = (half + core) % 2
        acc[other, spot] = acc[other, spot] + product
    out = [
        pltpu.make_async_copy(acc.at[1], send_ref, sems.at[1]),
        pltpu.make_async_copy(acc.at[0], keep_ref, sems.at[0]),
    ]
    for copy in out:
        copy.start()
    for copy in out:
        copy.wait()


def middle_kernel(parts_ref, weight_ref, cot_ref, output_ref, packet_ref):
    peers = parts_ref.shape[0]
    total = parts_ref[0]
    for peer in range(1, peers):
        total = total + parts_ref[peer]
    weight = weight_ref[...]
    pre = dot3(total, weight, ((1,), (0,)))
    sig = jax.nn.sigmoid(pre)
    output_ref[...] = pre * sig
    grad = cot_ref[...] * sig * (1.0 + pre * (1.0 - sig))
    moving = dot3(grad, weight, ((1,), (1,)))
    term = dot3(total, grad, ((0,), (0,)))
    size = moving.shape[0]
    share = packet_ref.shape[1] - size
    for peer in range(peers):
        packet_ref[peer, 0:size] = moving
        packet_ref[peer, size : size + share] = term[peer * share : (peer + 1) * share]


def backward_kernel(inner, index_ref, count_ref, tiles_ref, own_ref, other_ref, packet_ref):
    capacity, size = tiles_ref.shape[0], tiles_ref.shape[1]
    col_blocks = packet_ref.shape[0]
    share = packet_ref.shape[1] - size
    core = lax.axis_index("col") % 2
    packet_ref[:, 0:size] = jnp.zeros((col_blocks, size, packet_ref.shape[2]), jnp.float32)
    term = own_ref[0, size : size + share] + other_ref[0, size : size + share]
    for peer in range(1, own_ref.shape[0]):
        term = term + (own_ref[peer, size : size + share] + other_ref[peer, size : size + share])
    for block in range(col_blocks):
        packet_ref[block, size : size + share] = term
    for slot in range(capacity):
        place = index_ref[slot]
        row, col = place // col_blocks, place % col_blocks
        half, spot = half_place(row, inner)
        data = jnp.where(half == core, own_ref[spot, 0:size], other_ref[spot, 0:size])
        data = jnp.where(slot < count_ref[0], data, 0.0)
        high, low = split_bf16(data)
        tile = tiles_ref[slot]
        product = lax.dot_general(
            jnp.concatenate([tile, tile], axis=0),
            jnp.concatenate([high, low], axis=0),
            (((0,), (0,)), ((), ())),
            preferred_element_type=jnp.float32,
        )
        packet_ref[col, 0:size] = packet_ref[col, 0:size] + product


def on_device(features, weight, tile_values, tile_index, tile_counts, cotangent):
    tiles = tile_values.reshape(tile_values.shape[-3:])
    slot_index = tile_index.reshape(-1)
    live_count = tile_counts.reshape(-1)
    capacity, size, _ = tiles.shape
    width = features.shape[1]
    rows = lax.axis_size("row")
    cols = lax.axis_size("col")
    inner = lax.axis_size("depth")
    half = cols * inner // 2
    share = size // half
    node_total = size * rows * cols * inner
    swap = [(i, i ^ 1) for i in range(cols)]
    same_core = [[(z * 2 + c) * inner + x for z in range(cols // 2) for x in range(inner)] for c in range(2)]
    params = pltpu.CompilerParams(vmem_limit_bytes=MEM)
    smem = pl.BlockSpec(memory_space=pltpu.SMEM)
    vmem = pl.BlockSpec(memory_space=pltpu.VMEM)
    hbm = pl.BlockSpec(memory_space=pl.ANY)

    def swap_half(value):
        return lax.all_to_all(
            value, ("col", "depth"), 0, 0, tiled=True, axis_index_groups=same_core
        )

    spread = jnp.broadcast_to(features[None], (rows,) + features.shape)
    column_data = lax.all_to_all(spread, "row", 0, 0, tiled=True)
    block = jax.ShapeDtypeStruct((half, size, width), jnp.float32)
    keep, send = pl.pallas_call(
        functools.partial(forward_kernel, inner),
        out_shape=(block, block),
        in_specs=[smem, smem, vmem, vmem],
        out_specs=(hbm, hbm),
        scratch_shapes=[
            pltpu.VMEM((2, half, size, width), jnp.float32),
            pltpu.SemaphoreType.DMA((2,)),
        ],
        compiler_params=params,
        name="forward_tiles",
    )(slot_index, live_count, tiles, column_data)
    partial = keep + lax.ppermute(send, "col", swap)
    parts = swap_half(partial)
    output, packet = pl.pallas_call(
        middle_kernel,
        out_shape=(
            jax.ShapeDtypeStruct((size, width), jnp.float32),
            jax.ShapeDtypeStruct((half, size + share, width), jnp.float32),
        ),
        in_specs=[vmem, vmem, vmem],
        out_specs=(vmem, vmem),
        compiler_params=params,
        name="dense_layer",
    )(parts, weight, cotangent)
    own = swap_half(packet)
    other = lax.ppermute(own, "col", swap)
    back = pl.pallas_call(
        functools.partial(backward_kernel, inner),
        out_shape=jax.ShapeDtypeStruct((rows, size + share, width), jnp.float32),
        in_specs=[smem, smem, vmem, vmem, vmem],
        out_specs=vmem,
        compiler_params=params,
        name="backward_tiles",
    )(slot_index, live_count, tiles, own, other)
    landed = lax.all_to_all(back, "row", 0, 0, tiled=True)
    summed = landed.sum(axis=0)
    feature_grad = summed[:size]
    term = summed[size:] * (1.0 / math.sqrt(node_total))
    weight_grad = swap_half(jnp.broadcast_to(term[None], (half, share, width))).reshape(half * share, width)
    return (output, weight_grad, feature_grad)


def solution(mesh):
    return jax.shard_map(
        on_device,
        mesh=mesh,
        in_specs=(
            P(("row", "col", "depth"), None),
            P(),
            P("row", "col", "depth", None, None, None),
            P("row", "col", "depth", None),
            P("row", "col", "depth"),
            P(("row", "col", "depth"), None),
        ),
        out_specs=(P(("row", "col", "depth"), None), P(), P(("row", "col", "depth"), None)),
        check_vma=False,
    )
```

time: 841 us -> 182 us (0.22)
  the two profiles are of different devices: /device:TPU:2 before, /device:TPU:8 now
where the time goes in v1:
time: 182 us
  blocking collectives  106 us (58%)
  waiting for transfers between devices  43.3 us (24%)
  starting transfers between devices  23.8 us (13%)
  local copies, waits for them, and re-layouts  3.82 us (2%)
  Pallas kernels  3.37 us (2%)
    all_to_all x2, blocking collectives, swap_half(): lax.all_to_all(value, ('col', 'depth'), 0, 0, tiled=True, axis_index_grou...  65.8 us
    all_to_all x1, blocking collectives, on_device(): landed = lax.all_to_all(back, 'row', 0, 0, tiled=True)  40 us
    all_to_all x1, waiting for transfers between devices, on_device(): column_data = lax.all_to_all(spread, 'row', 0, 0, tiled=True)  30.2 us
    all_to_all x1, starting transfers between devices, on_device(): column_data = lax.all_to_all(spread, 'row', 0, 0, tiled=True)  16.1 us
    all_to_all x1, waiting for transfers between devices, swap_half(): lax.all_to_all(value, ('col', 'depth'), 0, 0, tiled=True, axis_index_grou...  7.77 us
    all_to_all x1, starting transfers between devices, swap_half(): lax.all_to_all(value, ('col', 'depth'), 0, 0, tiled=True, axis_index_grou...  3.79 us
  transfers between devices with their start and end apart: 4, of which 4 were waited for; matrix products, arithmetic and copies ran while one was open for 0% of the time, Pallas kernels for 0%

profile of v1, /device:TPU:8, one launch (start us, length us, event | category | flops | bytes accessed | tf_op | source)
XLA Modules:
  0.0 181.6 jit_solution(14057237585206511728)
XLA Ops:
  0.6 1.9 %broadcast_in_dim.4 = f32[16,128,128]{2,1,0:T(8,128)} broadcast(f32[128,128]{1,0:T(8,128)} %param.6), dimensions={1,2} | broadcast | bytes 1114112 | tf_op jit(solution)/shard_map/broadcast_in_dim | solution.py:134
  2.5 0.0 copy-start
  2.5 0.0 copy-start.3
  2.5 16.1 %all-to-all-start = ((f32[16,128,128]{2,1,0:T(8,128)}), f32[16,128,128]{2,1,0:T(8,128)S(1)}, u32[]{:S(2)}, u32[]{:S(2)}) async-start(f32[16,128,128]{2,1,0:T(8,128)} %broadcast_in_dim.4), calls=%async_computation | async-start | bytes 2097152 | tf_op jit(solution)/shard_map/all_to_all | solution.py:135
  19.3 30.2 %all-to-all-done.cols_ref = f32[16,128,128]{2,1,0:T(8,128)S(1)} async-done(((f32[16,128,128]{2,1,0:T(8,128)}), f32[16,128,128]{2,1,0:T(8,128)S(1)}, u32[]{:S(2)}, u32[]{:S(2)}) %all-to-all-start) | async-done | bytes 1048608 | tf_op jit(solution)/shard_map/all_to_all | solution.py:135
  49.5 0.0 copy-done
  49.5 0.0 copy-done.3
  49.5 1.4 forward_tiles.1
  50.9 1.9 %collective-permute-start = (f32[16,128,128]{2,1,0:T(8,128)S(1)}, f32[16,128,128]{2,1,0:T(8,128)S(1)}, u32[]{:S(2)}, u32[]{:S(2)}) collective-permute-start(f32[16,128,128]{2,1,0:T(8,128)S(1)} %get-tuple-element.8), channel_id=1, source_target_pairs={{0,4},{4,0},{8,12},{12,8},{16,20},{20,16},{24,28},{28,24},{1,5},{5... | collective-permute-start | bytes 3145736 | tf_op jit(solution)/shard_map/ppermute | solution.py:149
  52.8 2.6 %collective-permute-done = f32[16,128,128]{2,1,0:T(8,128)S(1)} collective-permute-done((f32[16,128,128]{2,1,0:T(8,128)S(1)}, f32[16,128,128]{2,1,0:T(8,128)S(1)}, u32[]{:S(2)}, u32[]{:S(2)}) %collective-permute-start) | collective-permute-done | bytes 1048608 | tf_op jit(solution)/shard_map/ppermute | solution.py:149
  55.4 0.1 add.3
  55.6 0.0 copy-start.1
  55.6 0.0 copy-start.2
  55.6 33.2 %all_to_all.25.parts_ref = f32[16,128,128]{2,1,0:T(8,128)S(1)} all-to-all(f32[16,128,128]{2,1,0:T(8,128)S(1)} %add.3), channel_id=1, replica_groups={{0,1,2,3,8,9,10,11,16,17,18,19,24,25,26,27},{4,5,6,7,12,13,14,15,20,21,..., dimensions={0} | all-to-all | bytes 2097152 | tf_op jit(solution)/shard_map/all_to_all | solution.py:130
  88.8 0.0 copy-done.1
  88.8 0.0 copy-done.2
  88.8 0.8 dense_layer.1
  89.6 32.6 %all_to_all.26.own_ref = f32[16,136,128]{2,1,0:T(8,128)S(1)} all-to-all(f32[16,136,128]{2,1,0:T(8,128)S(1)} %get-tuple-element.10), channel_id=1, replica_groups={{0,1,2,3,8,9,10,11,16,17,18,19,24,25,26,27},{4,5,6,7,12,13,14,15,20,21,..., dimensions={0} | all-to-all | bytes 2228224 | tf_op jit(solution)/shard_map/all_to_all | solution.py:130
  122.3 1.9 %collective-permute-start.1 = (f32[16,136,128]{2,1,0:T(8,128)S(1)}, f32[16,136,128]{2,1,0:T(8,128)S(1)}, u32[]{:S(2)}, u32[]{:S(2)}) collective-permute-start(f32[16,136,128]{2,1,0:T(8,128)S(1)} %all_to_all.26.own_ref), channel_id=1, source_target_pairs={{0,4},{4,0},{8,12},{12,8},{16,20},{20,16},{24,28},{28,24},{1,5},{5... | collective-permute-start | bytes 3342344 | tf_op jit(solution)/shard_map/ppermute | solution.py:163
  124.2 2.7 %collective-permute-done.1.other_ref = f32[16,136,128]{2,1,0:T(8,128)S(1)} collective-permute-done((f32[16,136,128]{2,1,0:T(8,128)S(1)}, f32[16,136,128]{2,1,0:T(8,128)S(1)}, u32[]{:S(2)}, u32[]{:S(2)}) %collective-permute-start.1) | collective-permute-done | bytes 1114144 | tf_op jit(solution)/shard_map/ppermute | solution.py:163
  126.9 1.1 backward_tiles.1
  128.0 40.0 %all_to_all.27 = f32[16,136,128]{2,1,0:T(8,128)S(1)} all-to-all(f32[16,136,128]{2,1,0:T(8,128)S(1)} %backward_tiles.1), channel_id=1, replica_groups=mesh['row'=16,'col'=8,'depth'=4] {'row'}, dimensions={0} | all-to-all | bytes 2228224 | tf_op jit(solution)/shard_map/all_to_all | solution.py:172
  168.1 0.1 reduce_sum.9
  168.2 0.6 broadcast_in_dim.5
  168.8 3.8 %all-to-all-start.4 = ((f32[16,8,128]{2,1,0:T(8,128)}), f32[16,8,128]{2,1,0:T(8,128)S(1)}, u32[]{:S(2)}, u32[]{:S(2)}) async-start(f32[16,8,128]{2,1,0:T(8,128)} %broadcast_in_dim.5), calls=%async_computation.4 | async-start | bytes 131072 | tf_op jit(solution)/shard_map/all_to_all | solution.py:130
  172.6 0.6 slice.9
  173.2 7.8 %all-to-all-done.4 = f32[16,8,128]{2,1,0:T(8,128)S(1)} async-done(((f32[16,8,128]{2,1,0:T(8,128)}), f32[16,8,128]{2,1,0:T(8,128)S(1)}, u32[]{:S(2)}, u32[]{:S(2)}) %all-to-all-start.4) | async-done | bytes 65568 | tf_op jit(solution)/shard_map/all_to_all | solution.py:130
  181.0 0.6 copy.11
  (1 shorter events, 0.0 us)
Async XLA Ops:
  2.5 47.0 %copy-start = (bf16[1,1,1,16,128,128]{5,4,3,2,1,0:T(8,128)(2,1)S(1)}, bf16[1,1,1,16,128,128]{5,4,3,2,1,0:T(8,128)(2,1)}, u32[]{:S(2)}) copy-start(bf16[1,1,1,16,128,128]{5,4,3,2,1,0:T(8,128)(2,1)} %param.8) | copy-start | bytes 1572868
  2.5 47.0 %copy-start.3 = (s32[1,1,1,16]{3,2,1,0:T(1,128)S(1)}, s32[1,1,1,16]{3,2,1,0:T(1,128)}, u32[]{:S(2)}) copy-start(s32[1,1,1,16]{3,2,1,0:T(1,128)} %param.9) | copy-start | bytes 196
  2.5 47.0 %all-to-all-start = ((f32[16,128,128]{2,1,0:T(8,128)}), f32[16,128,128]{2,1,0:T(8,128)S(1)}, u32[]{:S(2)}, u32[]{:S(2)}) async-start(f32[16,128,128]{2,1,0:T(8,128)} %broadcast_in_dim.4), calls=%async_computation | async-start | bytes 2097152 | tf_op jit(solution)/shard_map/all_to_all | solution.py:135
  50.9 4.6 %collective-permute-start = (f32[16,128,128]{2,1,0:T(8,128)S(1)}, f32[16,128,128]{2,1,0:T(8,128)S(1)}, u32[]{:S(2)}, u32[]{:S(2)}) collective-permute-start(f32[16,128,128]{2,1,0:T(8,128)S(1)} %get-tuple-element.8), channel_id=1, source_target_pairs={{0,4},{4,0},{8,12},{12,8},{16,20},{20,16},{24,28},{28,24},{1,5},{5... | collective-permute-start | bytes 3145736 | tf_op jit(solution)/shard_map/ppermute | solution.py:149
  55.6 33.2 %copy-start.1 = (f32[128,128]{1,0:T(8,128)S(1)}, f32[128,128]{1,0:T(8,128)}, u32[]{:S(2)}) copy-start(f32[128,128]{1,0:T(8,128)} %weight_ref.1) | copy-start | bytes 196612
  55.6 33.2 %copy-start.2 = (f32[128,128]{1,0:T(8,128)S(1)}, f32[128,128]{1,0:T(8,128)}, u32[]{:S(2)}) copy-start(f32[128,128]{1,0:T(8,128)} %cot_ref.1) | copy-start | bytes 196612
  122.3 4.6 %collective-permute-start.1 = (f32[16,136,128]{2,1,0:T(8,128)S(1)}, f32[16,136,128]{2,1,0:T(8,128)S(1)}, u32[]{:S(2)}, u32[]{:S(2)}) collective-permute-start(f32[16,136,128]{2,1,0:T(8,128)S(1)} %all_to_all.26.own_ref), channel_id=1, source_target_pairs={{0,4},{4,0},{8,12},{12,8},{16,20},{20,16},{24,28},{28,24},{1,5},{5... | collective-permute-start | bytes 3342344 | tf_op jit(solution)/shard_map/ppermute | solution.py:163
  168.8 12.2 %all-to-all-start.4 = ((f32[16,8,128]{2,1,0:T(8,128)}), f32[16,8,128]{2,1,0:T(8,128)S(1)}, u32[]{:S(2)}, u32[]{:S(2)}) async-start(f32[16,8,128]{2,1,0:T(8,128)} %broadcast_in_dim.5), calls=%async_computation.4 | async-start | bytes 131072 | tf_op jit(solution)/shard_map/all_to_all | solution.py:130

commit v2 on v1

v2 whole, which is shorter than its diff:
```python
import functools
import math

import jax
import jax.numpy as jnp
from jax import lax
from jax.experimental import pallas as pl
from jax.experimental.pallas import tpu as pltpu
from jax.sharding import PartitionSpec as P

MEM = 48 * 1024 * 1024
MIX = True
CD = ("col", "depth")


def split_bf16(value):
    high = value.astype(jnp.bfloat16)
    low = (value - high.astype(jnp.float32)).astype(jnp.bfloat16)
    return high, low


def dot3(left, right, dims):
    lh, ll = split_bf16(left)
    rh, rl = split_bf16(right)

    def one(a, b):
        return lax.dot_general(a, b, (dims, ((), ())), preferred_element_type=jnp.float32)

    return one(lh, rh) + (one(lh, rl) + one(ll, rh))


def half_place(block, inner, outer):
    half, run, step = (block // inner) % 2, block // (2 * inner), block % inner
    depth_first = step * outer + run
    if MIX:
        return half, jnp.where(half == 0, depth_first, run * inner + step)
    return half, depth_first


def tile_product(tile, data, transposed):
    high, low = split_bf16(data)
    axis = 0 if transposed else 1
    return lax.dot_general(
        jnp.concatenate([tile, tile], axis=axis),
        jnp.concatenate([high, low], axis=0),
        (((axis,), (0,)), ((), ())),
        preferred_element_type=jnp.float32,
    )


def spread_kernel(features_ref, spread_ref):
    data = features_ref[...]
    for peer in range(spread_ref.shape[0]):
        spread_ref[peer] = data


def forward_kernel(inner, outer, index_ref, count_ref, tiles_ref, cols_ref, keep_ref, send_ref, acc, sems):
    core = lax.axis_index("col") % 2
    blocks = cols_ref.shape[0]
    acc[...] = jnp.zeros_like(acc)
    for slot in range(tiles_ref.shape[0]):
        place = index_ref[slot]
        half, spot = half_place(place // blocks, inner, outer)
        data = jnp.where(slot < count_ref[0], cols_ref[place % blocks], 0.0)
        away = (half + core) % 2
        acc[away, spot] = acc[away, spot] + tile_product(tiles_ref[slot], data, False)
    out = [
        pltpu.make_async_copy(acc.at[1], send_ref, sems.at[1]),
        pltpu.make_async_copy(acc.at[0], keep_ref, sems.at[0]),
    ]
    for copy in out:
        copy.start()
    for copy in out:
        copy.wait()


def middle_kernel(inner, parts_ref, weight_ref, cot_ref, output_ref, packet_ref):
    core = lax.axis_index("col") % 2
    total = parts_ref[0]
    for peer in range(1, parts_ref.shape[0]):
        total = total + parts_ref[peer]
    weight = weight_ref[...]
    pre = dot3(total, weight, ((1,), (0,)))
    sig = jax.nn.sigmoid(pre)
    output_ref[...] = pre * sig
    grad = cot_ref[...] * sig * (1.0 + pre * (1.0 - sig))
    moving = dot3(grad, weight, ((1,), (1,)))
    term = dot3(total, grad, ((0,), (0,)))
    size = moving.shape[0]
    peers = packet_ref.shape[0]
    rows = size // (peers * inner)
    for peer in range(peers):
        packet_ref[peer, 0:size] = moving
        for step in range(inner):
            at = (peer * inner + step) * rows
            piece = term[at : at + rows]
            if MIX:
                at = (step * inner + peer) * rows
                piece = jnp.where(core == 0, piece, term[at : at + rows])
            packet_ref[peer, size + step * rows : size + (step + 1) * rows] = piece


def repack_kernel(landed_ref, packet_ref):
    outer, length = landed_ref.shape[0], landed_ref.shape[1]
    part, size = packet_ref.shape[1], landed_ref.shape[2]
    term = landed_ref[0, size:length]
    for peer in range(1, outer):
        term = term + landed_ref[peer, size:length]
    share = part - outer * size
    for peer in range(packet_ref.shape[0]):
        for piece in range(outer):
            packet_ref[peer, piece * size : (piece + 1) * size] = landed_ref[piece, 0:size]
        packet_ref[peer, outer * size : part] = term[peer * share : (peer + 1) * share]


def backward_kernel(inner, outer, index_ref, count_ref, tiles_ref, own_ref, other_ref, packet_ref):
    blocks = packet_ref.shape[0]
    size = tiles_ref.shape[1]
    core = lax.axis_index("col") % 2
    span = outer * size
    share = own_ref.shape[1] - span
    term = own_ref[0, span:] + other_ref[0, span:]
    for peer in range(1, own_ref.shape[0]):
        term = term + (own_ref[peer, span:] + other_ref[peer, span:])
    for block in range(blocks):
        packet_ref[block, 0:size] = jnp.zeros((size, packet_ref.shape[2]), jnp.float32)
        packet_ref[block, size : size + share] = term
    for slot in range(tiles_ref.shape[0]):
        place = index_ref[slot]
        col = place % blocks
        half, spot = half_place(place // blocks, inner, outer)
        at = pl.ds(pl.multiple_of((spot % outer) * size, size), size)
        data = jnp.where(half == core, own_ref[spot // outer, at], other_ref[spot // outer, at])
        data = jnp.where(slot < count_ref[0], data, 0.0)
        packet_ref[col, 0:size] = packet_ref[col, 0:size] + tile_product(tiles_ref[slot], data, True)


def last_kernel(scale, landed_ref, grad_ref, spread_ref):
    size = grad_ref.shape[0]
    total = landed_ref[0]
    for peer in range(1, landed_ref.shape[0]):
        total = total + landed_ref[peer]
    grad_ref[...] = total[0:size]
    for peer in range(spread_ref.shape[0]):
        spread_ref[peer] = total[size:] * scale


def on_device(features, weight, tile_values, tile_index, tile_counts, cotangent):
    tiles = tile_values.reshape(tile_values.shape[-3:])
    slot_index = tile_index.reshape(-1)
    live_count = tile_counts.reshape(-1)
    size, width = features.shape
    rows = lax.axis_size("row")
    cols = lax.axis_size("col")
    inner = lax.axis_size("depth")
    outer = cols // 2
    assert inner == outer
    half = outer * inner
    share = size // half
    node_total = size * rows * cols * inner
    swap = [(i, i ^ 1) for i in range(cols)]
    place = lambda z, c, x: (z * 2 + c) * inner + x
    along_depth = [[[place(z, c, x) for x in range(inner)] for z in range(outer)] for c in range(2)]
    along_col = [[[place(z, c, x) for z in range(outer)] for x in range(inner)] for c in range(2)]
    if MIX:
        large, small = along_depth[0] + along_col[1], along_col[0] + along_depth[1]
    else:
        large, small = along_depth[0] + along_depth[1], along_col[0] + along_col[1]
    same_core = [[place(z, c, x) for z in range(outer) for x in range(inner)] for c in range(2)]
    smem = pl.BlockSpec(memory_space=pltpu.SMEM)
    vmem = pl.BlockSpec(memory_space=pltpu.VMEM)
    hbm = pl.BlockSpec(memory_space=pl.ANY)

    def shape(*dims):
        return jax.ShapeDtypeStruct(dims + (width,), jnp.float32)

    def call(kernel, name, out_shape, in_specs, out_specs, scratch=()):
        return pl.pallas_call(
            kernel,
            out_shape=out_shape,
            in_specs=in_specs,
            out_specs=out_specs,
            scratch_shapes=scratch,
            compiler_params=pltpu.CompilerParams(vmem_limit_bytes=MEM),
            name=name,
        )

    def exchange(value, groups):
        return lax.all_to_all(value, CD, 0, 0, tiled=True, axis_index_groups=groups)

    spread = call(spread_kernel, "spread", shape(rows, size), [vmem], vmem)(features)
    columns = lax.all_to_all(spread, "row", 0, 0, tiled=True)
    keep, send = call(
        functools.partial(forward_kernel, inner, outer),
        "forward_tiles",
        (shape(half, size), shape(half, size)),
        [smem, smem, vmem, vmem],
        (hbm, hbm),
        [pltpu.VMEM((2, half, size, width), jnp.float32), pltpu.SemaphoreType.DMA((2,))],
    )(slot_index, live_count, tiles, columns)
    parts = keep + lax.ppermute(send, "col", swap)
    landed = exchange(parts.reshape(inner, outer * size, width), large)
    parts = exchange(landed.sum(axis=0).reshape(outer, size, width), small)
    output, packet = call(
        functools.partial(middle_kernel, inner),
        "dense_layer",
        (shape(size), shape(outer, size + size // outer)),
        [vmem, vmem, vmem],
        (vmem, vmem),
    )(parts, weight, cotangent)
    landed = exchange(packet, small)
    packet = call(repack_kernel, "repack", shape(inner, outer * size + share), [vmem], vmem)(landed)
    own = exchange(packet, large)
    other = lax.ppermute(own, "col", swap)
    back = call(
        functools.partial(backward_kernel, inner, outer),
        "backward_tiles",
        shape(rows, size + share),
        [smem, smem, vmem, vmem, vmem],
        vmem,
    )(slot_index, live_count, tiles, own, other)
    landed = lax.all_to_all(back, "row", 0, 0, tiled=True)
    feature_grad, spread = call(
        functools.partial(last_kernel, 1.0 / math.sqrt(node_total)),
        "add_landed",
        (shape(size), shape(half, share)),
        [vmem],
        (vmem, vmem),
    )(landed)
    weight_grad = exchange(spread, same_core).reshape(size, width)
    return (output, weight_grad, feature_grad)


def solution(mesh):
    return jax.shard_map(
        on_device,
        mesh=mesh,
        in_specs=(
            P(("row", "col", "depth"), None),
            P(),
            P("row", "col", "depth", None, None, None),
            P("row", "col", "depth", None),
            P("row", "col", "depth"),
            P(("row", "col", "depth"), None),
        ),
        out_specs=(P(("row", "col", "depth"), None), P(), P(("row", "col", "depth"), None)),
        check_vma=False,
    )
```

time: 182 us -> 169 us (0.929)
  waiting for transfers between devices: 43.3 us -> 35.1 us
  blocking collectives: 106 us -> 102 us
  local copies, waits for them, and re-layouts: 3.82 us -> 1.48 us
  Pallas kernels: 3.37 us -> 5.19 us
    all_to_all x2 -> x1, waiting for transfers between devices: 37.9 us -> 30.2 us  [on_device(): columns = lax.all_to_all(spread, 'row', 0, 0, tiled=True)]
    all_to_all x2 -> x5, blocking collectives: 65.8 us -> 61.3 us  [exchange(): return lax.all_to_all(value, CD, 0, 0, tiled=True, axis_index_groups=groups)]
    all_to_all x2 -> x1, starting transfers between devices: 19.9 us -> 16.1 us  [on_device(): columns = lax.all_to_all(spread, 'row', 0, 0, tiled=True)]
    ppermute x1, starting transfers between devices: 1.91 us -> 5.26 us  [on_device(): other = lax.ppermute(own, 'col', swap)]
    broadcast_in_dim x2 -> x0, local copies, waits for them, and re-layouts: 2.54 us -> none  [the longest x1 1.9 us: on_device(): spread = jnp.broadcast_to(features[None], (rows,) + features.shape)]
    pallas_call x3 -> x6, Pallas kernels: 3.37 us -> 5.19 us  [the longest x1 1.34 us: on_device(): call(functools.partial(forward_kernel, inner, outer), 'forward_tiles', (s...]
  transfers between devices with their start and end apart: 4 -> 3, of which waited for: 4 -> 3; matrix products, arithmetic and copies ran while one was open for 0% -> 0% of each run, Pallas kernels for 0% -> 0%
where the time goes in v2:
time: 169 us
  blocking collectives  102 us (60%)
  waiting for transfers between devices  35.1 us (21%)
  starting transfers between devices  23.3 us (14%)
  Pallas kernels  5.19 us (3%)
    all_to_all x5, blocking collectives, exchange(): return lax.all_to_all(value, CD, 0, 0, tiled=True, axis_index_groups=groups)  61.3 us
    all_to_all x1, blocking collectives, on_device(): landed = lax.all_to_all(back, 'row', 0, 0, tiled=True)  40.7 us
    all_to_all x1, waiting for transfers between devices, on_device(): columns = lax.all_to_all(spread, 'row', 0, 0, tiled=True)  30.2 us
    all_to_all x1, starting transfers between devices, on_device(): columns = lax.all_to_all(spread, 'row', 0, 0, tiled=True)  16.1 us
    ppermute x1, starting transfers between devices, on_device(): other = lax.ppermute(own, 'col', swap)  5.26 us
  transfers between devices with their start and end apart: 3, of which 3 were waited for; matrix products, arithmetic and copies ran while one was open for 0% of the time, Pallas kernels for 0%

profile of v2, /device:TPU:8, one launch (start us, length us, event | category | flops | bytes accessed | tf_op | source)
XLA Modules:
  0.0 168.6 jit_solution(9239656638781188866)
XLA Ops:
  0.6 0.0 copy-start.1
  0.6 0.8 copy-done.1
  1.5 1.1 spread.1
  2.5 0.0 copy-start
  2.5 0.0 copy-start.4
  2.5 16.1 %all-to-all-start = ((f32[16,128,128]{2,1,0:T(8,128)}), f32[16,128,128]{2,1,0:T(8,128)S(1)}, u32[]{:S(2)}, u32[]{:S(2)}) async-start(f32[16,128,128]{2,1,0:T(8,128)} %spread.1), calls=%async_computation | async-start | bytes 2097152 | tf_op jit(solution)/shard_map/all_to_all | solution.py:192
  19.3 30.2 %all-to-all-done.cols_ref = f32[16,128,128]{2,1,0:T(8,128)S(1)} async-done(((f32[16,128,128]{2,1,0:T(8,128)}), f32[16,128,128]{2,1,0:T(8,128)S(1)}, u32[]{:S(2)}, u32[]{:S(2)}) %all-to-all-start) | async-done | bytes 1048608 | tf_op jit(solution)/shard_map/all_to_all | solution.py:192
  49.5 0.0 copy-done
  49.5 0.0 copy-done.4
  49.5 1.3 forward_tiles.1
  50.9 1.9 %collective-permute-start = (f32[16,128,128]{2,1,0:T(8,128)S(1)}, f32[16,128,128]{2,1,0:T(8,128)S(1)}, u32[]{:S(2)}, u32[]{:S(2)}) collective-permute-start(f32[16,128,128]{2,1,0:T(8,128)S(1)} %get-tuple-element.10), channel_id=1, source_target_pairs={{0,4},{4,0},{8,12},{12,8},{16,20},{20,16},{24,28},{28,24},{1,5},{5... | collective-permute-start | bytes 3145736 | tf_op jit(solution)/shard_map/ppermute | solution.py:201
  52.8 2.6 %collective-permute-done = f32[16,128,128]{2,1,0:T(8,128)S(1)} collective-permute-done((f32[16,128,128]{2,1,0:T(8,128)S(1)}, f32[16,128,128]{2,1,0:T(8,128)S(1)}, u32[]{:S(2)}, u32[]{:S(2)}) %collective-permute-start) | collective-permute-done | bytes 1048608 | tf_op jit(solution)/shard_map/ppermute | solution.py:201
  55.4 0.1 add.3
  55.5 15.0 %all_to_all.35 = f32[4,512,128]{2,1,0:T(8,128)S(1)} all-to-all(f32[4,512,128]{2,1,0:T(8,128)S(1)} %bitcast.12), channel_id=1, replica_groups={{0,1,2,3},{8,9,10,11},{16,17,18,19},{24,25,26,27},{4,12,20,28},{5,13,21..., dimensions={0} | all-to-all | bytes 2097152 | tf_op jit(solution)/shard_map/all_to_all | solution.py:189
  70.5 0.0 copy-start.2
  70.5 0.0 copy-start.3
  70.5 0.1 reduce_sum.9
  70.6 10.7 %all_to_all.36.parts_ref = f32[4,128,128]{2,1,0:T(8,128)S(1)} all-to-all(f32[4,128,128]{2,1,0:T(8,128)S(1)} %bitcast.13), channel_id=1, replica_groups={{0,8,16,24},{1,9,17,25},{2,10,18,26},{3,11,19,27},{4,5,6,7},{12,13,14,1..., dimensions={0} | all-to-all | bytes 524288 | tf_op jit(solution)/shard_map/all_to_all | solution.py:189
  81.3 0.0 copy-done.2
  81.3 0.0 copy-done.3
  81.3 0.8 dense_layer.1
  82.1 10.7 %all_to_all.37.landed_ref = f32[4,160,128]{2,1,0:T(8,128)S(1)} all-to-all(f32[4,160,128]{2,1,0:T(8,128)S(1)} %get-tuple-element.12), channel_id=1, replica_groups={{0,8,16,24},{1,9,17,25},{2,10,18,26},{3,11,19,27},{4,5,6,7},{12,13,14,1..., dimensions={0} | all-to-all | bytes 655360 | tf_op jit(solution)/shard_map/all_to_all | solution.py:189
  92.8 0.1 repack.1
  92.8 13.4 %all_to_all.38.own_ref = f32[4,520,128]{2,1,0:T(8,128)S(1)} all-to-all(f32[4,520,128]{2,1,0:T(8,128)S(1)} %repack.1), channel_id=1, replica_groups={{0,1,2,3},{8,9,10,11},{16,17,18,19},{24,25,26,27},{4,12,20,28},{5,13,21..., dimensions={0} | all-to-all | bytes 2129920 | tf_op jit(solution)/shard_map/all_to_all | solution.py:189
  106.2 5.3 %collective-permute-start.1 = (f32[4,520,128]{2,1,0:T(8,128)S(1)}, f32[4,520,128]{2,1,0:T(8,128)S(1)}, u32[]{:S(2)}, u32[]{:S(2)}) collective-permute-start(f32[4,520,128]{2,1,0:T(8,128)S(1)} %all_to_all.38.own_ref), channel_id=1, source_target_pairs={{0,4},{4,0},{8,12},{12,8},{16,20},{20,16},{24,28},{28,24},{1,5},{5... | collective-permute-start | bytes 3194888 | tf_op jit(solution)/shard_map/ppermute | solution.py:214
  111.5 2.3 %collective-permute-done.1.other_ref = f32[4,520,128]{2,1,0:T(8,128)S(1)} collective-permute-done((f32[4,520,128]{2,1,0:T(8,128)S(1)}, f32[4,520,128]{2,1,0:T(8,128)S(1)}, u32[]{:S(2)}, u32[]{:S(2)}) %collective-permute-start.1) | collective-permute-done | bytes 1064992 | tf_op jit(solution)/shard_map/ppermute | solution.py:214
  113.8 1.2 backward_tiles.1
  115.0 40.7 %all_to_all.39.landed_ref = f32[16,136,128]{2,1,0:T(8,128)S(1)} all-to-all(f32[16,136,128]{2,1,0:T(8,128)S(1)} %backward_tiles.1), channel_id=1, replica_groups=mesh['row'=16,'col'=8,'depth'=4] {'row'}, dimensions={0} | all-to-all | bytes 2228224 | tf_op jit(solution)/shard_map/all_to_all | solution.py:222
  155.6 0.7 add_landed.1
  156.3 11.6 %all_to_all.40 = f32[16,8,128]{2,1,0:T(8,128)S(1)} all-to-all(f32[16,8,128]{2,1,0:T(8,128)S(1)} %get-tuple-element.13), channel_id=1, replica_groups={{0,1,2,3,8,9,10,11,16,17,18,19,24,25,26,27},{4,5,6,7,12,13,14,15,20,21,..., dimensions={0} | all-to-all | bytes 131072 | tf_op jit(solution)/shard_map/all_to_all | solution.py:189
  168.0 0.6 copy.11
Async XLA Ops:
  0.6 0.8 copy-start.1
  2.5 47.0 %copy-start = (bf16[1,1,1,16,128,128]{5,4,3,2,1,0:T(8,128)(2,1)S(1)}, bf16[1,1,1,16,128,128]{5,4,3,2,1,0:T(8,128)(2,1)}, u32[]{:S(2)}) copy-start(bf16[1,1,1,16,128,128]{5,4,3,2,1,0:T(8,128)(2,1)} %param.8) | copy-start | bytes 1572868
  2.5 47.0 %copy-start.4 = (s32[1,1,1,16]{3,2,1,0:T(1,128)S(1)}, s32[1,1,1,16]{3,2,1,0:T(1,128)}, u32[]{:S(2)}) copy-start(s32[1,1,1,16]{3,2,1,0:T(1,128)} %param.9) | copy-start | bytes 196
  2.5 47.0 %all-to-all-start = ((f32[16,128,128]{2,1,0:T(8,128)}), f32[16,128,128]{2,1,0:T(8,128)S(1)}, u32[]{:S(2)}, u32[]{:S(2)}) async-start(f32[16,128,128]{2,1,0:T(8,128)} %spread.1), calls=%async_computation | async-start | bytes 2097152 | tf_op jit(solution)/shard_map/all_to_all | solution.py:192
  50.9 4.6 %collective-permute-start = (f32[16,128,128]{2,1,0:T(8,128)S(1)}, f32[16,128,128]{2,1,0:T(8,128)S(1)}, u32[]{:S(2)}, u32[]{:S(2)}) collective-permute-start(f32[16,128,128]{2,1,0:T(8,128)S(1)} %get-tuple-element.10), channel_id=1, source_target_pairs={{0,4},{4,0},{8,12},{12,8},{16,20},{20,16},{24,28},{28,24},{1,5},{5... | collective-permute-start | bytes 3145736 | tf_op jit(solution)/shard_map/ppermute | solution.py:201
  70.5 10.7 %copy-start.2 = (f32[128,128]{1,0:T(8,128)S(1)}, f32[128,128]{1,0:T(8,128)}, u32[]{:S(2)}) copy-start(f32[128,128]{1,0:T(8,128)} %weight_ref.1) | copy-start | bytes 196612
  70.5 10.7 %copy-start.3 = (f32[128,128]{1,0:T(8,128)S(1)}, f32[128,128]{1,0:T(8,128)}, u32[]{:S(2)}) copy-start(f32[128,128]{1,0:T(8,128)} %cot_ref.1) | copy-start | bytes 196612
  106.2 7.6 %collective-permute-start.1 = (f32[4,520,128]{2,1,0:T(8,128)S(1)}, f32[4,520,128]{2,1,0:T(8,128)S(1)}, u32[]{:S(2)}, u32[]{:S(2)}) collective-permute-start(f32[4,520,128]{2,1,0:T(8,128)S(1)} %all_to_all.38.own_ref), channel_id=1, source_target_pairs={{0,4},{4,0},{8,12},{12,8},{16,20},{20,16},{24,28},{28,24},{1,5},{5... | collective-permute-start | bytes 3194888 | tf_op jit(solution)/shard_map/ppermute | solution.py:214

commit v3 on v2

--- a/solution.py
+++ b/solution.py
@@ -9,7 +9,8 @@
 from jax.sharding import PartitionSpec as P
 
 MEM = 48 * 1024 * 1024
-MIX = True
+TURN = 8
+ZFAST = True
 CD = ("col", "depth")
 
 
@@ -32,9 +33,7 @@
 def half_place(block, inner, outer):
     half, run, step = (block // inner) % 2, block // (2 * inner), block % inner
     depth_first = step * outer + run
-    if MIX:
-        return half, jnp.where(half == 0, depth_first, run * inner + step)
-    return half, depth_first
+    return half, jnp.where(half == 0, depth_first, run * inner + step)
 
 
 def tile_product(tile, data, transposed):
@@ -48,30 +47,27 @@
     )
 
 
-def spread_kernel(features_ref, spread_ref):
-    data = features_ref[...]
-    for peer in range(spread_ref.shape[0]):
-        spread_ref[peer] = data
-
-
-def forward_kernel(inner, outer, index_ref, count_ref, tiles_ref, cols_ref, keep_ref, send_ref, acc, sems):
+def parity_place(block):
+    if ZFAST:
+        return block % 2, ((block % TURN) // 2) * 2 + block // TURN
+    return block % 2, (block // TURN) * (TURN // 2) + (block % TURN) // 2
+
+
+def forward_kernel(inner, outer, blocks, index_ref, count_ref, tiles_ref, near_ref, far_ref, keep_ref, send_ref):
     core = lax.axis_index("col") % 2
-    blocks = cols_ref.shape[0]
-    acc[...] = jnp.zeros_like(acc)
+    mine = lax.axis_index("row") % 2
+    keep_ref[...] = jnp.zeros_like(keep_ref)
+    send_ref[...] = jnp.zeros_like(send_ref)
     for slot in range(tiles_ref.shape[0]):
         place = index_ref[slot]
         half, spot = half_place(place // blocks, inner, outer)
-        data = jnp.where(slot < count_ref[0], cols_ref[place % blocks], 0.0)
-        away = (half + core) % 2
-        acc[away, spot] = acc[away, spot] + tile_product(tiles_ref[slot], data, False)
-    out = [
-        pltpu.make_async_copy(acc.at[1], send_ref, sems.at[1]),
-        pltpu.make_async_copy(acc.at[0], keep_ref, sems.at[0]),
-    ]
-    for copy in out:
-        copy.start()
-    for copy in out:
-        copy.wait()
+        parity, at = parity_place(place % blocks)
+        data = jnp.where(parity == mine, near_ref[at], far_ref[at])
+        data = jnp.where(slot < count_ref[0], data, 0.0)
+        product = tile_product(tiles_ref[slot], data, False)
+        kept = half == core
+        keep_ref[spot] = keep_ref[spot] + jnp.where(kept, product, 0.0)
+        send_ref[spot] = send_ref[spot] + jnp.where(kept, 0.0, product)
 
 
 def middle_kernel(inner, parts_ref, weight_ref, cot_ref, output_ref, packet_ref):
@@ -94,9 +90,8 @@
         for step in range(inner):
             at = (peer * inner + step) * rows
             piece = term[at : at + rows]
-            if MIX:
-                at = (step * inner + peer) * rows
-                piece = jnp.where(core == 0, piece, term[at : at + rows])
+            at = (step * inner + peer) * rows
+            piece = jnp.where(core == 0, piece, term[at : at + rows])
             packet_ref[peer, size + step * rows : size + (step + 1) * rows] = piece
 
 
@@ -113,26 +108,32 @@
         packet_ref[peer, outer * size : part] = term[peer * share : (peer + 1) * share]
 
 
-def backward_kernel(inner, outer, index_ref, count_ref, tiles_ref, own_ref, other_ref, packet_ref):
-    blocks = packet_ref.shape[0]
+def backward_kernel(
+    inner, outer, blocks, index_ref, count_ref, tiles_ref, own_ref, other_ref, keep_ref, away_ref
+):
     size = tiles_ref.shape[1]
     core = lax.axis_index("col") % 2
+    mine = lax.axis_index("row") % 2
     span = outer * size
-    share = own_ref.shape[1] - span
     term = own_ref[0, span:] + other_ref[0, span:]
     for peer in range(1, own_ref.shape[0]):
         term = term + (own_ref[peer, span:] + other_ref[peer, span:])
-    for block in range(blocks):
-        packet_ref[block, 0:size] = jnp.zeros((size, packet_ref.shape[2]), jnp.float32)
-        packet_ref[block, size : size + share] = term
+    zero = jnp.zeros((size, keep_ref.shape[2]), jnp.float32)
+    for block in range(keep_ref.shape[0]):
+        for ref in (keep_ref, away_ref):
+            ref[block, 0:size] = zero
+            ref[block, size:] = term
     for slot in range(tiles_ref.shape[0]):
         place = index_ref[slot]
-        col = place % blocks
         half, spot = half_place(place // blocks, inner, outer)
+        parity, to = parity_place(place % blocks)
         at = pl.ds(pl.multiple_of((spot % outer) * size, size), size)
         data = jnp.where(half == core, own_ref[spot // outer, at], other_ref[spot // outer, at])
         data = jnp.where(slot < count_ref[0], data, 0.0)
-        packet_ref[col, 0:size] = packet_ref[col, 0:size] + tile_product(tiles_ref[slot], data, True)
+        product = tile_product(tiles_ref[slot], data, True)
+        kept = parity == mine
+        keep_ref[to, 0:size] = keep_ref[to, 0:size] + jnp.where(kept, product, 0.0)
+        away_ref[to, 0:size] = away_ref[to, 0:size] + jnp.where(kept, 0.0, product)
 
 
 def last_kernel(scale, landed_ref, grad_ref, spread_ref):
@@ -162,14 +163,19 @@
     place = lambda z, c, x: (z * 2 + c) * inner + x
     along_depth = [[[place(z, c, x) for x in range(inner)] for z in range(outer)] for c in range(2)]
     along_col = [[[place(z, c, x) for z in range(outer)] for x in range(inner)] for c in range(2)]
-    if MIX:
-        large, small = along_depth[0] + along_col[1], along_col[0] + along_depth[1]
+    large, small = along_depth[0] + along_col[1], along_col[0] + along_depth[1]
+    def beside(row, core):
+        base, y = row - row % TURN, row % TURN
+        return base + (y + (1 if (y + core) % 2 == 0 else -1)) % TURN
+
+    if ZFAST:
+        same_parity = [[z + y for y in range(p, TURN, 2) for z in range(0, rows, TURN)] for p in range(2)]
     else:
-        large, small = along_depth[0] + along_depth[1], along_col[0] + along_col[1]
+        same_parity = [[z + y for z in range(0, rows, TURN) for y in range(p, TURN, 2)] for p in range(2)]
+    neighbour = [(y * cols + c, beside(y, c % 2) * cols + c) for y in range(rows) for c in range(cols)]
     same_core = [[place(z, c, x) for z in range(outer) for x in range(inner)] for c in range(2)]
     smem = pl.BlockSpec(memory_space=pltpu.SMEM)
     vmem = pl.BlockSpec(memory_space=pltpu.VMEM)
-    hbm = pl.BlockSpec(memory_space=pl.ANY)
 
     def shape(*dims):
         return jax.ShapeDtypeStruct(dims + (width,), jnp.float32)
@@ -188,16 +194,16 @@
     def exchange(value, groups):
         return lax.all_to_all(value, CD, 0, 0, tiled=True, axis_index_groups=groups)
 
-    spread = call(spread_kernel, "spread", shape(rows, size), [vmem], vmem)(features)
-    columns = lax.all_to_all(spread, "row", 0, 0, tiled=True)
+    spread = jnp.broadcast_to(features[None], (rows // 2, size, width))
+    near = lax.all_to_all(spread, "row", 0, 0, tiled=True, axis_index_groups=same_parity)
+    far = lax.ppermute(near, ("row", "col"), neighbour)
     keep, send = call(
-        functools.partial(forward_kernel, inner, outer),
+        functools.partial(forward_kernel, inner, outer, rows),
         "forward_tiles",
         (shape(half, size), shape(half, size)),
-        [smem, smem, vmem, vmem],
-        (hbm, hbm),
-        [pltpu.VMEM((2, half, size, width), jnp.float32), pltpu.SemaphoreType.DMA((2,))],
-    )(slot_index, live_count, tiles, columns)
+        [smem, smem, vmem, vmem, vmem],
+        (vmem, vmem),
+    )(slot_index, live_count, tiles, near, far)
     parts = keep + lax.ppermute(send, "col", swap)
     landed = exchange(parts.reshape(inner, outer * size, width), large)
     parts = exchange(landed.sum(axis=0).reshape(outer, size, width), small)
@@ -212,14 +218,15 @@
     packet = call(repack_kernel, "repack", shape(inner, outer * size + share), [vmem], vmem)(landed)
     own = exchange(packet, large)
     other = lax.ppermute(own, "col", swap)
-    back = call(
-        functools.partial(backward_kernel, inner, outer),
+    keep, away = call(
+        functools.partial(backward_kernel, inner, outer, rows),
         "backward_tiles",
-        shape(rows, size + share),
+        (shape(rows // 2, size + share),) * 2,
         [smem, smem, vmem, vmem, vmem],
-        vmem,
+        (vmem, vmem),
     )(slot_index, live_count, tiles, own, other)
-    landed = lax.all_to_all(back, "row", 0, 0, tiled=True)
+    moved = keep + lax.ppermute(away, ("row", "col"), neighbour)
+    landed = lax.all_to_all(moved, "row", 0, 0, tiled=True, axis_index_groups=same_parity)
     feature_grad, spread = call(
         functools.partial(last_kernel, 1.0 / math.sqrt(node_total)),
         "add_landed",

time: 169 us -> 165 us (0.976)
  the two profiles are of different devices: /device:TPU:8 before, /device:TPU:16 now
where the time goes in v3:
time: 165 us
  blocking collectives  123 us (75%)
  waiting for transfers between devices  22.9 us (14%)
  starting transfers between devices  11 us (7%)
  Pallas kernels  4.17 us (3%)
    all_to_all x5, blocking collectives, exchange(): return lax.all_to_all(value, CD, 0, 0, tiled=True, axis_index_groups=groups)  61.9 us
    all_to_all x1, blocking collectives, on_device(): lax.all_to_all(spread, 'row', 0, 0, tiled=True, axis_index_groups=same_pa...  36.2 us
    all_to_all x1, blocking collectives, on_device(): lax.all_to_all(moved, 'row', 0, 0, tiled=True, axis_index_groups=same_par...  25.3 us
    ppermute x1, waiting for transfers between devices, on_device(): moved = keep + lax.ppermute(away, ('row', 'col'), neighbour)  9.5 us
    ppermute x1, waiting for transfers between devices, on_device(): far = lax.ppermute(near, ('row', 'col'), neighbour)  8.5 us
    ppermute x1, starting transfers between devices, on_device(): other = lax.ppermute(own, 'col', swap)  5.26 us
  transfers between devices with their start and end apart: 4, of which 4 were waited for; matrix products, arithmetic and copies ran while one was open for 0% of the time, Pallas kernels for 0%

profile of v3, /device:TPU:16, one launch (start us, length us, event | category | flops | bytes accessed | tf_op | source)
XLA Modules:
  0.0 164.6 jit_solution(2478228841111055987)
XLA Ops:
  0.6 0.0 copy-start.3
  0.6 0.0 copy-start
  0.7 0.9 broadcast_in_dim.2
  1.6 36.2 %all_to_all.35.near_ref = f32[8,128,128]{2,1,0:T(8,128)S(1)} all-to-all(f32[8,128,128]{2,1,0:T(8,128)S(1)} %broadcast_in_dim.2), channel_id=1, replica_groups={{0,256,64,320,128,384,192,448},{32,288,96,352,160,416,224,480},{1,257,6..., dimensions={0} | all-to-all | bytes 1048576 | tf_op jit(solution)/shard_map/all_to_all | solution.py:198
  37.7 1.9 %collective-permute-start = (f32[8,128,128]{2,1,0:T(8,128)S(1)}, f32[8,128,128]{2,1,0:T(8,128)S(1)}, u32[]{:S(2)}, u32[]{:S(2)}) collective-permute-start(f32[8,128,128]{2,1,0:T(8,128)S(1)} %all_to_all.35.near_ref), channel_id=1, source_target_pairs={{0,32},{4,228},{8,40},{12,236},{16,48},{20,244},{24,56},{28,252},{... | collective-permute-start | bytes 1572872 | tf_op jit(solution)/shard_map/ppermute | solution.py:199
  40.3 8.5 %collective-permute-done.far_ref = f32[8,128,128]{2,1,0:T(8,128)S(1)} collective-permute-done((f32[8,128,128]{2,1,0:T(8,128)S(1)}, f32[8,128,128]{2,1,0:T(8,128)S(1)}, u32[]{:S(2)}, u32[]{:S(2)}) %collective-permute-start) | collective-permute-done | bytes 524320 | tf_op jit(solution)/shard_map/ppermute | solution.py:199
  48.8 0.0 copy-done.3
  48.8 0.0 copy-done
  48.8 1.3 forward_tiles.1
  50.1 1.9 %collective-permute-start.1 = (f32[16,128,128]{2,1,0:T(8,128)S(1)}, f32[16,128,128]{2,1,0:T(8,128)S(1)}, u32[]{:S(2)}, u32[]{:S(2)}) collective-permute-start(f32[16,128,128]{2,1,0:T(8,128)S(1)} %get-tuple-element.12), channel_id=1, source_target_pairs={{0,4},{4,0},{8,12},{12,8},{16,20},{20,16},{24,28},{28,24},{1,5},{5... | collective-permute-start | bytes 3145736 | tf_op jit(solution)/shard_map/ppermute | solution.py:207
  52.1 2.6 %collective-permute-done.1 = f32[16,128,128]{2,1,0:T(8,128)S(1)} collective-permute-done((f32[16,128,128]{2,1,0:T(8,128)S(1)}, f32[16,128,128]{2,1,0:T(8,128)S(1)}, u32[]{:S(2)}, u32[]{:S(2)}) %collective-permute-start.1) | collective-permute-done | bytes 1048608 | tf_op jit(solution)/shard_map/ppermute | solution.py:207
  54.7 0.1 add.6
  54.8 15.0 %all_to_all.36 = f32[4,512,128]{2,1,0:T(8,128)S(1)} all-to-all(f32[4,512,128]{2,1,0:T(8,128)S(1)} %bitcast.12), channel_id=1, replica_groups={{0,1,2,3},{8,9,10,11},{16,17,18,19},{24,25,26,27},{4,12,20,28},{5,13,21..., dimensions={0} | all-to-all | bytes 2097152 | tf_op jit(solution)/shard_map/all_to_all | solution.py:195
  69.8 0.0 copy-start.1
  69.8 0.0 copy-start.2
  69.8 0.1 reduce_sum.9
  69.9 10.9 %all_to_all.37.parts_ref = f32[4,128,128]{2,1,0:T(8,128)S(1)} all-to-all(f32[4,128,128]{2,1,0:T(8,128)S(1)} %bitcast.13), channel_id=1, replica_groups={{0,8,16,24},{1,9,17,25},{2,10,18,26},{3,11,19,27},{4,5,6,7},{12,13,14,1..., dimensions={0} | all-to-all | bytes 524288 | tf_op jit(solution)/shard_map/all_to_all | solution.py:195
  80.8 0.0 copy-done.1
  80.8 0.0 copy-done.2
  80.8 0.8 dense_layer.1
  81.7 10.7 %all_to_all.38.landed_ref = f32[4,160,128]{2,1,0:T(8,128)S(1)} all-to-all(f32[4,160,128]{2,1,0:T(8,128)S(1)} %get-tuple-element.14), channel_id=1, replica_groups={{0,8,16,24},{1,9,17,25},{2,10,18,26},{3,11,19,27},{4,5,6,7},{12,13,14,1..., dimensions={0} | all-to-all | bytes 655360 | tf_op jit(solution)/shard_map/all_to_all | solution.py:195
  92.3 0.1 repack.1
  92.4 13.4 %all_to_all.39.own_ref = f32[4,520,128]{2,1,0:T(8,128)S(1)} all-to-all(f32[4,520,128]{2,1,0:T(8,128)S(1)} %repack.1), channel_id=1, replica_groups={{0,1,2,3},{8,9,10,11},{16,17,18,19},{24,25,26,27},{4,12,20,28},{5,13,21..., dimensions={0} | all-to-all | bytes 2129920 | tf_op jit(solution)/shard_map/all_to_all | solution.py:195
  105.8 5.3 %collective-permute-start.2 = (f32[4,520,128]{2,1,0:T(8,128)S(1)}, f32[4,520,128]{2,1,0:T(8,128)S(1)}, u32[]{:S(2)}, u32[]{:S(2)}) collective-permute-start(f32[4,520,128]{2,1,0:T(8,128)S(1)} %all_to_all.39.own_ref), channel_id=1, source_target_pairs={{0,4},{4,0},{8,12},{12,8},{16,20},{20,16},{24,28},{28,24},{1,5},{5... | collective-permute-start | bytes 3194888 | tf_op jit(solution)/shard_map/ppermute | solution.py:220
  111.0 2.3 %collective-permute-done.2.other_ref = f32[4,520,128]{2,1,0:T(8,128)S(1)} collective-permute-done((f32[4,520,128]{2,1,0:T(8,128)S(1)}, f32[4,520,128]{2,1,0:T(8,128)S(1)}, u32[]{:S(2)}, u32[]{:S(2)}) %collective-permute-start.2) | collective-permute-done | bytes 1064992 | tf_op jit(solution)/shard_map/ppermute | solution.py:220
  113.3 1.3 backward_tiles.1
  114.6 1.9 %collective-permute-start.3 = (f32[8,136,128]{2,1,0:T(8,128)S(1)}, f32[8,136,128]{2,1,0:T(8,128)S(1)}, u32[]{:S(2)}, u32[]{:S(2)}) collective-permute-start(f32[8,136,128]{2,1,0:T(8,128)S(1)} %get-tuple-element.16), channel_id=1, source_target_pairs={{0,32},{4,228},{8,40},{12,236},{16,48},{20,244},{24,56},{28,252},{... | collective-permute-start | bytes 1671176 | tf_op jit(solution)/shard_map/ppermute | solution.py:228
  116.6 9.5 %collective-permute-done.3 = f32[8,136,128]{2,1,0:T(8,128)S(1)} collective-permute-done((f32[8,136,128]{2,1,0:T(8,128)S(1)}, f32[8,136,128]{2,1,0:T(8,128)S(1)}, u32[]{:S(2)}, u32[]{:S(2)}) %collective-permute-start.3) | collective-permute-done | bytes 557088 | tf_op jit(solution)/shard_map/ppermute | solution.py:228
  126.1 0.1 add.7
  126.1 25.3 %all_to_all.40.landed_ref = f32[8,136,128]{2,1,0:T(8,128)S(1)} all-to-all(f32[8,136,128]{2,1,0:T(8,128)S(1)} %add.7), channel_id=1, replica_groups={{0,256,64,320,128,384,192,448},{32,288,96,352,160,416,224,480},{1,257,6..., dimensions={0} | all-to-all | bytes 1114112 | tf_op jit(solution)/shard_map/all_to_all | solution.py:229
  151.4 0.7 add_landed.1
  152.1 12.0 %all_to_all.41 = f32[16,8,128]{2,1,0:T(8,128)S(1)} all-to-all(f32[16,8,128]{2,1,0:T(8,128)S(1)} %get-tuple-element.17), channel_id=1, replica_groups={{0,1,2,3,8,9,10,11,16,17,18,19,24,25,26,27},{4,5,6,7,12,13,14,15,20,21,..., dimensions={0} | all-to-all | bytes 131072 | tf_op jit(solution)/shard_map/all_to_all | solution.py:195
  164.0 0.6 copy.11
Async XLA Ops:
  0.6 48.2 %copy-start.3 = (s32[1,1,1,16]{3,2,1,0:T(1,128)S(1)}, s32[1,1,1,16]{3,2,1,0:T(1,128)}, u32[]{:S(2)}) copy-start(s32[1,1,1,16]{3,2,1,0:T(1,128)} %param.9) | copy-start | bytes 196
  0.6 48.2 %copy-start = (bf16[1,1,1,16,128,128]{5,4,3,2,1,0:T(8,128)(2,1)S(1)}, bf16[1,1,1,16,128,128]{5,4,3,2,1,0:T(8,128)(2,1)}, u32[]{:S(2)}) copy-start(bf16[1,1,1,16,128,128]{5,4,3,2,1,0:T(8,128)(2,1)} %param.8) | copy-start | bytes 1572868
  37.7 11.1 %collective-permute-start = (f32[8,128,128]{2,1,0:T(8,128)S(1)}, f32[8,128,128]{2,1,0:T(8,128)S(1)}, u32[]{:S(2)}, u32[]{:S(2)}) collective-permute-start(f32[8,128,128]{2,1,0:T(8,128)S(1)} %all_to_all.35.near_ref), channel_id=1, source_target_pairs={{0,32},{4,228},{8,40},{12,236},{16,48},{20,244},{24,56},{28,252},{... | collective-permute-start | bytes 1572872 | tf_op jit(solution)/shard_map/ppermute | solution.py:199
  50.1 4.6 %collective-permute-start.1 = (f32[16,128,128]{2,1,0:T(8,128)S(1)}, f32[16,128,128]{2,1,0:T(8,128)S(1)}, u32[]{:S(2)}, u32[]{:S(2)}) collective-permute-start(f32[16,128,128]{2,1,0:T(8,128)S(1)} %get-tuple-element.12), channel_id=1, source_target_pairs={{0,4},{4,0},{8,12},{12,8},{16,20},{20,16},{24,28},{28,24},{1,5},{5... | collective-permute-start | bytes 3145736 | tf_op jit(solution)/shard_map/ppermute | solution.py:207
  69.8 11.0 %copy-start.1 = (f32[128,128]{1,0:T(8,128)S(1)}, f32[128,128]{1,0:T(8,128)}, u32[]{:S(2)}) copy-start(f32[128,128]{1,0:T(8,128)} %weight_ref.1) | copy-start | bytes 196612
  69.8 11.0 %copy-start.2 = (f32[128,128]{1,0:T(8,128)S(1)}, f32[128,128]{1,0:T(8,128)}, u32[]{:S(2)}) copy-start(f32[128,128]{1,0:T(8,128)} %cot_ref.1) | copy-start | bytes 196612
  105.8 7.6 %collective-permute-start.2 = (f32[4,520,128]{2,1,0:T(8,128)S(1)}, f32[4,520,128]{2,1,0:T(8,128)S(1)}, u32[]{:S(2)}, u32[]{:S(2)}) collective-permute-start(f32[4,520,128]{2,1,0:T(8,128)S(1)} %all_to_all.39.own_ref), channel_id=1, source_target_pairs={{0,4},{4,0},{8,12},{12,8},{16,20},{20,16},{24,28},{28,24},{1,5},{5... | collective-permute-start | bytes 3194888 | tf_op jit(solution)/shard_map/ppermute | solution.py:220
  114.6 11.4 %collective-permute-start.3 = (f32[8,136,128]{2,1,0:T(8,128)S(1)}, f32[8,136,128]{2,1,0:T(8,128)S(1)}, u32[]{:S(2)}, u32[]{:S(2)}) collective-permute-start(f32[8,136,128]{2,1,0:T(8,128)S(1)} %get-tuple-element.16), channel_id=1, source_target_pairs={{0,32},{4,228},{8,40},{12,236},{16,48},{20,244},{24,56},{28,252},{... | collective-permute-start | bytes 1671176 | tf_op jit(solution)/shard_map/ppermute | solution.py:228

commit v4 on v3

--- a/solution.py
+++ b/solution.py
@@ -10,7 +10,6 @@
 
 MEM = 48 * 1024 * 1024
 TURN = 8
-ZFAST = True
 CD = ("col", "depth")
 
 
@@ -30,8 +29,14 @@
     return one(lh, rh) + (one(lh, rl) + one(ll, rh))
 
 
+def turned(at):
+    return at ^ (at // 2)
+
+
 def half_place(block, inner, outer):
     half, run, step = (block // inner) % 2, block // (2 * inner), block % inner
+    run = turned(run)
+    step = turned(step)
     depth_first = step * outer + run
     return half, jnp.where(half == 0, depth_first, run * inner + step)
 
@@ -48,9 +53,7 @@
 
 
 def parity_place(block):
-    if ZFAST:
-        return block % 2, ((block % TURN) // 2) * 2 + block // TURN
-    return block % 2, (block // TURN) * (TURN // 2) + (block % TURN) // 2
+    return block % 2, ((block % TURN) // 2) * 2 + block // TURN
 
 
 def forward_kernel(inner, outer, blocks, index_ref, count_ref, tiles_ref, near_ref, far_ref, keep_ref, send_ref):
@@ -161,19 +164,16 @@
     node_total = size * rows * cols * inner
     swap = [(i, i ^ 1) for i in range(cols)]
     place = lambda z, c, x: (z * 2 + c) * inner + x
-    along_depth = [[[place(z, c, x) for x in range(inner)] for z in range(outer)] for c in range(2)]
-    along_col = [[[place(z, c, x) for z in range(outer)] for x in range(inner)] for c in range(2)]
+    along_depth = [[[place(z, c, x) for x in map(turned, range(inner))] for z in map(turned, range(outer))] for c in range(2)]
+    along_col = [[[place(z, c, x) for z in map(turned, range(outer))] for x in map(turned, range(inner))] for c in range(2)]
     large, small = along_depth[0] + along_col[1], along_col[0] + along_depth[1]
     def beside(row, core):
         base, y = row - row % TURN, row % TURN
         return base + (y + (1 if (y + core) % 2 == 0 else -1)) % TURN
 
-    if ZFAST:
-        same_parity = [[z + y for y in range(p, TURN, 2) for z in range(0, rows, TURN)] for p in range(2)]
-    else:
-        same_parity = [[z + y for z in range(0, rows, TURN) for y in range(p, TURN, 2)] for p in range(2)]
+    same_parity = [[z + y for y in range(p, TURN, 2) for z in range(0, rows, TURN)] for p in range(2)]
     neighbour = [(y * cols + c, beside(y, c % 2) * cols + c) for y in range(rows) for c in range(cols)]
-    same_core = [[place(z, c, x) for z in range(outer) for x in range(inner)] for c in range(2)]
+    same_core = [[place(z, c, x) for z in map(turned, range(outer)) for x in map(turned, range(inner))] for c in range(2)]
     smem = pl.BlockSpec(memory_space=pltpu.SMEM)
     vmem = pl.BlockSpec(memory_space=pltpu.VMEM)
 

time: 165 us -> 165 us (level)
  no operation moved by 1% of the time
where the time goes in v4:
time: 165 us; the launch traced here: 164 us
  blocking collectives  123 us (75%)
  waiting for transfers between devices  22.9 us (14%)
  starting transfers between devices  10.1 us (6%)
  Pallas kernels  4.35 us (3%)
    all_to_all x5, blocking collectives, exchange(): return lax.all_to_all(value, CD, 0, 0, tiled=True, axis_index_groups=groups)  62 us
    all_to_all x1, blocking collectives, on_device(): lax.all_to_all(spread, 'row', 0, 0, tiled=True, axis_index_groups=same_pa...  36.2 us
    all_to_all x1, blocking collectives, on_device(): lax.all_to_all(moved, 'row', 0, 0, tiled=True, axis_index_groups=same_par...  25.3 us
    ppermute x1, waiting for transfers between devices, on_device(): moved = keep + lax.ppermute(away, ('row', 'col'), neighbour)  9.49 us
    ppermute x1, waiting for transfers between devices, on_device(): far = lax.ppermute(near, ('row', 'col'), neighbour)  8.5 us
    ppermute x1, starting transfers between devices, on_device(): other = lax.ppermute(own, 'col', swap)  4.38 us
  transfers between devices with their start and end apart: 4, of which 4 were waited for; matrix products, arithmetic and copies ran while one was open for 0% of the time, Pallas kernels for 0%

profile of v4, /device:TPU:16, one launch (start us, length us, event | category | flops | bytes accessed | tf_op | source)
XLA Modules:
  0.0 164.0 jit_solution(12085988382180619082)
XLA Ops:
  0.6 0.0 copy-start.3
  0.6 0.0 copy-start
  0.7 0.9 broadcast_in_dim.2
  1.6 36.2 %all_to_all.35.near_ref = f32[8,128,128]{2,1,0:T(8,128)S(1)} all-to-all(f32[8,128,128]{2,1,0:T(8,128)S(1)} %broadcast_in_dim.2), channel_id=1, replica_groups={{0,256,64,320,128,384,192,448},{32,288,96,352,160,416,224,480},{1,257,6..., dimensions={0} | all-to-all | bytes 1048576 | tf_op jit(solution)/shard_map/all_to_all | solution.py:198
  37.7 1.9 %collective-permute-start = (f32[8,128,128]{2,1,0:T(8,128)S(1)}, f32[8,128,128]{2,1,0:T(8,128)S(1)}, u32[]{:S(2)}, u32[]{:S(2)}) collective-permute-start(f32[8,128,128]{2,1,0:T(8,128)S(1)} %all_to_all.35.near_ref), channel_id=1, source_target_pairs={{0,32},{4,228},{8,40},{12,236},{16,48},{20,244},{24,56},{28,252},{... | collective-permute-start | bytes 1572872 | tf_op jit(solution)/shard_map/ppermute | solution.py:199
  40.3 8.5 %collective-permute-done.far_ref = f32[8,128,128]{2,1,0:T(8,128)S(1)} collective-permute-done((f32[8,128,128]{2,1,0:T(8,128)S(1)}, f32[8,128,128]{2,1,0:T(8,128)S(1)}, u32[]{:S(2)}, u32[]{:S(2)}) %collective-permute-start) | collective-permute-done | bytes 524320 | tf_op jit(solution)/shard_map/ppermute | solution.py:199
  48.8 0.0 copy-done.3
  48.8 0.0 copy-done
  48.8 1.4 forward_tiles.1
  50.2 1.9 %collective-permute-start.1 = (f32[16,128,128]{2,1,0:T(8,128)S(1)}, f32[16,128,128]{2,1,0:T(8,128)S(1)}, u32[]{:S(2)}, u32[]{:S(2)}) collective-permute-start(f32[16,128,128]{2,1,0:T(8,128)S(1)} %get-tuple-element.12), channel_id=1, source_target_pairs={{0,4},{4,0},{8,12},{12,8},{16,20},{20,16},{24,28},{28,24},{1,5},{5... | collective-permute-start | bytes 3145736 | tf_op jit(solution)/shard_map/ppermute | solution.py:207
  52.1 2.6 %collective-permute-done.1 = f32[16,128,128]{2,1,0:T(8,128)S(1)} collective-permute-done((f32[16,128,128]{2,1,0:T(8,128)S(1)}, f32[16,128,128]{2,1,0:T(8,128)S(1)}, u32[]{:S(2)}, u32[]{:S(2)}) %collective-permute-start.1) | collective-permute-done | bytes 1048608 | tf_op jit(solution)/shard_map/ppermute | solution.py:207
  54.8 0.1 add.6
  54.9 14.7 %all_to_all.36 = f32[4,512,128]{2,1,0:T(8,128)S(1)} all-to-all(f32[4,512,128]{2,1,0:T(8,128)S(1)} %bitcast.12), channel_id=1, replica_groups={{0,1,3,2},{8,9,11,10},{24,25,27,26},{16,17,19,18},{4,12,28,20},{5,13,29..., dimensions={0} | all-to-all | bytes 2097152 | tf_op jit(solution)/shard_map/all_to_all | solution.py:195
  69.6 0.0 copy-start.1
  69.6 0.0 copy-start.2
  69.6 0.1 reduce_sum.9
  69.7 11.5 %all_to_all.37.parts_ref = f32[4,128,128]{2,1,0:T(8,128)S(1)} all-to-all(f32[4,128,128]{2,1,0:T(8,128)S(1)} %bitcast.13), channel_id=1, replica_groups={{0,8,24,16},{1,9,25,17},{3,11,27,19},{2,10,26,18},{4,5,7,6},{12,13,15,1..., dimensions={0} | all-to-all | bytes 524288 | tf_op jit(solution)/shard_map/all_to_all | solution.py:195
  81.2 0.0 copy-done.1
  81.2 0.0 copy-done.2
  81.2 0.8 dense_layer.1
  82.0 10.6 %all_to_all.38.landed_ref = f32[4,160,128]{2,1,0:T(8,128)S(1)} all-to-all(f32[4,160,128]{2,1,0:T(8,128)S(1)} %get-tuple-element.14), channel_id=1, replica_groups={{0,8,24,16},{1,9,25,17},{3,11,27,19},{2,10,26,18},{4,5,7,6},{12,13,15,1..., dimensions={0} | all-to-all | bytes 655360 | tf_op jit(solution)/shard_map/all_to_all | solution.py:195
  92.6 0.1 repack.1
  92.6 13.3 %all_to_all.39.own_ref = f32[4,520,128]{2,1,0:T(8,128)S(1)} all-to-all(f32[4,520,128]{2,1,0:T(8,128)S(1)} %repack.1), channel_id=1, replica_groups={{0,1,3,2},{8,9,11,10},{24,25,27,26},{16,17,19,18},{4,12,28,20},{5,13,29..., dimensions={0} | all-to-all | bytes 2129920 | tf_op jit(solution)/shard_map/all_to_all | solution.py:195
  106.0 4.4 %collective-permute-start.2 = (f32[4,520,128]{2,1,0:T(8,128)S(1)}, f32[4,520,128]{2,1,0:T(8,128)S(1)}, u32[]{:S(2)}, u32[]{:S(2)}) collective-permute-start(f32[4,520,128]{2,1,0:T(8,128)S(1)} %all_to_all.39.own_ref), channel_id=1, source_target_pairs={{0,4},{4,0},{8,12},{12,8},{16,20},{20,16},{24,28},{28,24},{1,5},{5... | collective-permute-start | bytes 3194888 | tf_op jit(solution)/shard_map/ppermute | solution.py:220
  110.4 2.3 %collective-permute-done.2.other_ref = f32[4,520,128]{2,1,0:T(8,128)S(1)} collective-permute-done((f32[4,520,128]{2,1,0:T(8,128)S(1)}, f32[4,520,128]{2,1,0:T(8,128)S(1)}, u32[]{:S(2)}, u32[]{:S(2)}) %collective-permute-start.2) | collective-permute-done | bytes 1064992 | tf_op jit(solution)/shard_map/ppermute | solution.py:220
  112.6 1.4 backward_tiles.1
  114.1 1.9 %collective-permute-start.3 = (f32[8,136,128]{2,1,0:T(8,128)S(1)}, f32[8,136,128]{2,1,0:T(8,128)S(1)}, u32[]{:S(2)}, u32[]{:S(2)}) collective-permute-start(f32[8,136,128]{2,1,0:T(8,128)S(1)} %get-tuple-element.16), channel_id=1, source_target_pairs={{0,32},{4,228},{8,40},{12,236},{16,48},{20,244},{24,56},{28,252},{... | collective-permute-start | bytes 1671176 | tf_op jit(solution)/shard_map/ppermute | solution.py:228
  116.0 9.5 %collective-permute-done.3 = f32[8,136,128]{2,1,0:T(8,128)S(1)} collective-permute-done((f32[8,136,128]{2,1,0:T(8,128)S(1)}, f32[8,136,128]{2,1,0:T(8,128)S(1)}, u32[]{:S(2)}, u32[]{:S(2)}) %collective-permute-start.3) | collective-permute-done | bytes 557088 | tf_op jit(solution)/shard_map/ppermute | solution.py:228
  125.5 0.1 add.7
  125.6 25.3 %all_to_all.40.landed_ref = f32[8,136,128]{2,1,0:T(8,128)S(1)} all-to-all(f32[8,136,128]{2,1,0:T(8,128)S(1)} %add.7), channel_id=1, replica_groups={{0,256,64,320,128,384,192,448},{32,288,96,352,160,416,224,480},{1,257,6..., dimensions={0} | all-to-all | bytes 1114112 | tf_op jit(solution)/shard_map/all_to_all | solution.py:229
  150.8 0.7 add_landed.1
  151.5 11.9 %all_to_all.41 = f32[16,8,128]{2,1,0:T(8,128)S(1)} all-to-all(f32[16,8,128]{2,1,0:T(8,128)S(1)} %get-tuple-element.17), channel_id=1, replica_groups={{0,1,3,2,8,9,11,10,24,25,27,26,16,17,19,18},{4,5,7,6,12,13,15,14,28,29,..., dimensions={0} | all-to-all | bytes 131072 | tf_op jit(solution)/shard_map/all_to_all | solution.py:195
  163.4 0.6 copy.11
Async XLA Ops:
  0.6 48.2 %copy-start.3 = (s32[1,1,1,16]{3,2,1,0:T(1,128)S(1)}, s32[1,1,1,16]{3,2,1,0:T(1,128)}, u32[]{:S(2)}) copy-start(s32[1,1,1,16]{3,2,1,0:T(1,128)} %param.9) | copy-start | bytes 196
  0.6 48.2 %copy-start = (bf16[1,1,1,16,128,128]{5,4,3,2,1,0:T(8,128)(2,1)S(1)}, bf16[1,1,1,16,128,128]{5,4,3,2,1,0:T(8,128)(2,1)}, u32[]{:S(2)}) copy-start(bf16[1,1,1,16,128,128]{5,4,3,2,1,0:T(8,128)(2,1)} %param.8) | copy-start | bytes 1572868
  37.7 11.1 %collective-permute-start = (f32[8,128,128]{2,1,0:T(8,128)S(1)}, f32[8,128,128]{2,1,0:T(8,128)S(1)}, u32[]{:S(2)}, u32[]{:S(2)}) collective-permute-start(f32[8,128,128]{2,1,0:T(8,128)S(1)} %all_to_all.35.near_ref), channel_id=1, source_target_pairs={{0,32},{4,228},{8,40},{12,236},{16,48},{20,244},{24,56},{28,252},{... | collective-permute-start | bytes 1572872 | tf_op jit(solution)/shard_map/ppermute | solution.py:199
  50.2 4.6 %collective-permute-start.1 = (f32[16,128,128]{2,1,0:T(8,128)S(1)}, f32[16,128,128]{2,1,0:T(8,128)S(1)}, u32[]{:S(2)}, u32[]{:S(2)}) collective-permute-start(f32[16,128,128]{2,1,0:T(8,128)S(1)} %get-tuple-element.12), channel_id=1, source_target_pairs={{0,4},{4,0},{8,12},{12,8},{16,20},{20,16},{24,28},{28,24},{1,5},{5... | collective-permute-start | bytes 3145736 | tf_op jit(solution)/shard_map/ppermute | solution.py:207
  69.6 11.6 %copy-start.1 = (f32[128,128]{1,0:T(8,128)S(1)}, f32[128,128]{1,0:T(8,128)}, u32[]{:S(2)}) copy-start(f32[128,128]{1,0:T(8,128)} %weight_ref.1) | copy-start | bytes 196612
  69.6 11.6 %copy-start.2 = (f32[128,128]{1,0:T(8,128)S(1)}, f32[128,128]{1,0:T(8,128)}, u32[]{:S(2)}) copy-start(f32[128,128]{1,0:T(8,128)} %cot_ref.1) | copy-start | bytes 196612
  106.0 6.7 %collective-permute-start.2 = (f32[4,520,128]{2,1,0:T(8,128)S(1)}, f32[4,520,128]{2,1,0:T(8,128)S(1)}, u32[]{:S(2)}, u32[]{:S(2)}) collective-permute-start(f32[4,520,128]{2,1,0:T(8,128)S(1)} %all_to_all.39.own_ref), channel_id=1, source_target_pairs={{0,4},{4,0},{8,12},{12,8},{16,20},{20,16},{24,28},{28,24},{1,5},{5... | collective-permute-start | bytes 3194888 | tf_op jit(solution)/shard_map/ppermute | solution.py:220
  114.1 11.4 %collective-permute-start.3 = (f32[8,136,128]{2,1,0:T(8,128)S(1)}, f32[8,136,128]{2,1,0:T(8,128)S(1)}, u32[]{:S(2)}, u32[]{:S(2)}) collective-permute-start(f32[8,136,128]{2,1,0:T(8,128)S(1)} %get-tuple-element.16), channel_id=1, source_target_pairs={{0,32},{4,228},{8,40},{12,236},{16,48},{20,244},{24,56},{28,252},{... | collective-permute-start | bytes 1671176 | tf_op jit(solution)/shard_map/ppermute | solution.py:228

commit v5 on v4

--- a/solution.py
+++ b/solution.py
@@ -56,7 +56,7 @@
     return block % 2, ((block % TURN) // 2) * 2 + block // TURN
 
 
-def forward_kernel(inner, outer, blocks, index_ref, count_ref, tiles_ref, near_ref, far_ref, keep_ref, send_ref):
+def forward_kernel(inner, outer, blocks, index_ref, count_ref, tiles_ref, near_ref, far_ref, keep_ref, send_ref, prod_ref):
     core = lax.axis_index("col") % 2
     mine = lax.axis_index("row") % 2
     keep_ref[...] = jnp.zeros_like(keep_ref)
@@ -67,7 +67,10 @@
         parity, at = parity_place(place % blocks)
         data = jnp.where(parity == mine, near_ref[at], far_ref[at])
         data = jnp.where(slot < count_ref[0], data, 0.0)
-        product = tile_product(tiles_ref[slot], data, False)
+        prod_ref[slot] = tile_product(tiles_ref[slot], data, False)
+    for slot in range(tiles_ref.shape[0]):
+        half, spot = half_place(index_ref[slot] // blocks, inner, outer)
+        product = prod_ref[slot]
         kept = half == core
         keep_ref[spot] = keep_ref[spot] + jnp.where(kept, product, 0.0)
         send_ref[spot] = send_ref[spot] + jnp.where(kept, 0.0, product)
@@ -112,7 +115,7 @@
 
 
 def backward_kernel(
-    inner, outer, blocks, index_ref, count_ref, tiles_ref, own_ref, other_ref, keep_ref, away_ref
+    inner, outer, blocks, index_ref, count_ref, tiles_ref, own_ref, other_ref, keep_ref, away_ref, prod_ref
 ):
     size = tiles_ref.shape[1]
     core = lax.axis_index("col") % 2
@@ -129,11 +132,13 @@
     for slot in range(tiles_ref.shape[0]):
         place = index_ref[slot]
         half, spot = half_place(place // blocks, inner, outer)
-        parity, to = parity_place(place % blocks)
         at = pl.ds(pl.multiple_of((spot % outer) * size, size), size)
         data = jnp.where(half == core, own_ref[spot // outer, at], other_ref[spot // outer, at])
         data = jnp.where(slot < count_ref[0], data, 0.0)
-        product = tile_product(tiles_ref[slot], data, True)
+        prod_ref[slot] = tile_product(tiles_ref[slot], data, True)
+    for slot in range(tiles_ref.shape[0]):
+        parity, to = parity_place(index_ref[slot] % blocks)
+        product = prod_ref[slot]
         kept = parity == mine
         keep_ref[to, 0:size] = keep_ref[to, 0:size] + jnp.where(kept, product, 0.0)
         away_ref[to, 0:size] = away_ref[to, 0:size] + jnp.where(kept, 0.0, product)
@@ -153,6 +158,7 @@
     tiles = tile_values.reshape(tile_values.shape[-3:])
     slot_index = tile_index.reshape(-1)
     live_count = tile_counts.reshape(-1)
+    capacity = tiles.shape[0]
     size, width = features.shape
     rows = lax.axis_size("row")
     cols = lax.axis_size("col")
@@ -203,6 +209,7 @@
         (shape(half, size), shape(half, size)),
         [smem, smem, vmem, vmem, vmem],
         (vmem, vmem),
+        [pltpu.VMEM((capacity, size, width), jnp.float32)],
     )(slot_index, live_count, tiles, near, far)
     parts = keep + lax.ppermute(send, "col", swap)
     landed = exchange(parts.reshape(inner, outer * size, width), large)
@@ -224,6 +231,7 @@
         (shape(rows // 2, size + share),) * 2,
         [smem, smem, vmem, vmem, vmem],
         (vmem, vmem),
+        [pltpu.VMEM((capacity, size, width), jnp.float32)],
     )(slot_index, live_count, tiles, own, other)
     moved = keep + lax.ppermute(away, ("row", "col"), neighbour)
     landed = lax.all_to_all(moved, "row", 0, 0, tiled=True, axis_index_groups=same_parity)

time: 165 us -> 165 us (level)
  no operation moved by 1% of the time
where the time goes in v5:
time: 165 us; the launch traced here: 164 us
  blocking collectives  123 us (75%)
  waiting for transfers between devices  22.9 us (14%)
  starting transfers between devices  10.1 us (6%)
  Pallas kernels  4.43 us (3%)
    all_to_all x5, blocking collectives, exchange(): return lax.all_to_all(value, CD, 0, 0, tiled=True, axis_index_groups=groups)  62 us
    all_to_all x1, blocking collectives, on_device(): lax.all_to_all(spread, 'row', 0, 0, tiled=True, axis_index_groups=same_pa...  36.2 us
    all_to_all x1, blocking collectives, on_device(): lax.all_to_all(moved, 'row', 0, 0, tiled=True, axis_index_groups=same_par...  25.3 us
    ppermute x1, waiting for transfers between devices, on_device(): moved = keep + lax.ppermute(away, ('row', 'col'), neighbour)  9.5 us
    ppermute x1, waiting for transfers between devices, on_device(): far = lax.ppermute(near, ('row', 'col'), neighbour)  8.5 us
    ppermute x1, starting transfers between devices, on_device(): other = lax.ppermute(own, 'col', swap)  4.38 us
  transfers between devices with their start and end apart: 4, of which 4 were waited for; matrix products, arithmetic and copies ran while one was open for 0% of the time, Pallas kernels for 0%

profile of v5, /device:TPU:16, one launch (start us, length us, event | category | flops | bytes accessed | tf_op | source)
XLA Modules:
  0.0 164.1 jit_solution(17519508323501495229)
XLA Ops:
  0.6 0.0 copy-start.3
  0.6 0.0 copy-start
  0.7 0.9 broadcast_in_dim.2
  1.6 36.2 %all_to_all.35.near_ref = f32[8,128,128]{2,1,0:T(8,128)S(1)} all-to-all(f32[8,128,128]{2,1,0:T(8,128)S(1)} %broadcast_in_dim.2), channel_id=1, replica_groups={{0,256,64,320,128,384,192,448},{32,288,96,352,160,416,224,480},{1,257,6..., dimensions={0} | all-to-all | bytes 1048576 | tf_op jit(solution)/shard_map/all_to_all | solution.py:204
  37.7 1.9 %collective-permute-start = (f32[8,128,128]{2,1,0:T(8,128)S(1)}, f32[8,128,128]{2,1,0:T(8,128)S(1)}, u32[]{:S(2)}, u32[]{:S(2)}) collective-permute-start(f32[8,128,128]{2,1,0:T(8,128)S(1)} %all_to_all.35.near_ref), channel_id=1, source_target_pairs={{0,32},{4,228},{8,40},{12,236},{16,48},{20,244},{24,56},{28,252},{... | collective-permute-start | bytes 1572872 | tf_op jit(solution)/shard_map/ppermute | solution.py:205
  40.3 8.5 %collective-permute-done.far_ref = f32[8,128,128]{2,1,0:T(8,128)S(1)} collective-permute-done((f32[8,128,128]{2,1,0:T(8,128)S(1)}, f32[8,128,128]{2,1,0:T(8,128)S(1)}, u32[]{:S(2)}, u32[]{:S(2)}) %collective-permute-start) | collective-permute-done | bytes 524320 | tf_op jit(solution)/shard_map/ppermute | solution.py:205
  48.8 0.0 copy-done.3
  48.8 0.0 copy-done
  48.8 1.4 forward_tiles.1
  50.3 1.9 %collective-permute-start.1 = (f32[16,128,128]{2,1,0:T(8,128)S(1)}, f32[16,128,128]{2,1,0:T(8,128)S(1)}, u32[]{:S(2)}, u32[]{:S(2)}) collective-permute-start(f32[16,128,128]{2,1,0:T(8,128)S(1)} %get-tuple-element.12), channel_id=1, source_target_pairs={{0,4},{4,0},{8,12},{12,8},{16,20},{20,16},{24,28},{28,24},{1,5},{5... | collective-permute-start | bytes 3145736 | tf_op jit(solution)/shard_map/ppermute | solution.py:214
  52.2 2.6 %collective-permute-done.1 = f32[16,128,128]{2,1,0:T(8,128)S(1)} collective-permute-done((f32[16,128,128]{2,1,0:T(8,128)S(1)}, f32[16,128,128]{2,1,0:T(8,128)S(1)}, u32[]{:S(2)}, u32[]{:S(2)}) %collective-permute-start.1) | collective-permute-done | bytes 1048608 | tf_op jit(solution)/shard_map/ppermute | solution.py:214
  54.8 0.1 add.6
  55.0 14.7 %all_to_all.36 = f32[4,512,128]{2,1,0:T(8,128)S(1)} all-to-all(f32[4,512,128]{2,1,0:T(8,128)S(1)} %bitcast.12), channel_id=1, replica_groups={{0,1,3,2},{8,9,11,10},{24,25,27,26},{16,17,19,18},{4,12,28,20},{5,13,29..., dimensions={0} | all-to-all | bytes 2097152 | tf_op jit(solution)/shard_map/all_to_all | solution.py:201
  69.7 0.0 copy-start.1
  69.7 0.0 copy-start.2
  69.7 0.1 reduce_sum.9
  69.7 11.5 %all_to_all.37.parts_ref = f32[4,128,128]{2,1,0:T(8,128)S(1)} all-to-all(f32[4,128,128]{2,1,0:T(8,128)S(1)} %bitcast.13), channel_id=1, replica_groups={{0,8,24,16},{1,9,25,17},{3,11,27,19},{2,10,26,18},{4,5,7,6},{12,13,15,1..., dimensions={0} | all-to-all | bytes 524288 | tf_op jit(solution)/shard_map/all_to_all | solution.py:201
  81.2 0.0 copy-done.1
  81.2 0.0 copy-done.2
  81.2 0.8 dense_layer.1
  82.1 10.6 %all_to_all.38.landed_ref = f32[4,160,128]{2,1,0:T(8,128)S(1)} all-to-all(f32[4,160,128]{2,1,0:T(8,128)S(1)} %get-tuple-element.14), channel_id=1, replica_groups={{0,8,24,16},{1,9,25,17},{3,11,27,19},{2,10,26,18},{4,5,7,6},{12,13,15,1..., dimensions={0} | all-to-all | bytes 655360 | tf_op jit(solution)/shard_map/all_to_all | solution.py:201
  92.6 0.1 repack.1
  92.7 13.3 %all_to_all.39.own_ref = f32[4,520,128]{2,1,0:T(8,128)S(1)} all-to-all(f32[4,520,128]{2,1,0:T(8,128)S(1)} %repack.1), channel_id=1, replica_groups={{0,1,3,2},{8,9,11,10},{24,25,27,26},{16,17,19,18},{4,12,28,20},{5,13,29..., dimensions={0} | all-to-all | bytes 2129920 | tf_op jit(solution)/shard_map/all_to_all | solution.py:201
  106.0 4.4 %collective-permute-start.2 = (f32[4,520,128]{2,1,0:T(8,128)S(1)}, f32[4,520,128]{2,1,0:T(8,128)S(1)}, u32[]{:S(2)}, u32[]{:S(2)}) collective-permute-start(f32[4,520,128]{2,1,0:T(8,128)S(1)} %all_to_all.39.own_ref), channel_id=1, source_target_pairs={{0,4},{4,0},{8,12},{12,8},{16,20},{20,16},{24,28},{28,24},{1,5},{5... | collective-permute-start | bytes 3194888 | tf_op jit(solution)/shard_map/ppermute | solution.py:227
  110.4 2.3 %collective-permute-done.2.other_ref = f32[4,520,128]{2,1,0:T(8,128)S(1)} collective-permute-done((f32[4,520,128]{2,1,0:T(8,128)S(1)}, f32[4,520,128]{2,1,0:T(8,128)S(1)}, u32[]{:S(2)}, u32[]{:S(2)}) %collective-permute-start.2) | collective-permute-done | bytes 1064992 | tf_op jit(solution)/shard_map/ppermute | solution.py:227
  112.7 1.4 backward_tiles.1
  114.1 1.9 %collective-permute-start.3 = (f32[8,136,128]{2,1,0:T(8,128)S(1)}, f32[8,136,128]{2,1,0:T(8,128)S(1)}, u32[]{:S(2)}, u32[]{:S(2)}) collective-permute-start(f32[8,136,128]{2,1,0:T(8,128)S(1)} %get-tuple-element.16), channel_id=1, source_target_pairs={{0,32},{4,228},{8,40},{12,236},{16,48},{20,244},{24,56},{28,252},{... | collective-permute-start | bytes 1671176 | tf_op jit(solution)/shard_map/ppermute | solution.py:236
  116.1 9.5 %collective-permute-done.3 = f32[8,136,128]{2,1,0:T(8,128)S(1)} collective-permute-done((f32[8,136,128]{2,1,0:T(8,128)S(1)}, f32[8,136,128]{2,1,0:T(8,128)S(1)}, u32[]{:S(2)}, u32[]{:S(2)}) %collective-permute-start.3) | collective-permute-done | bytes 557088 | tf_op jit(solution)/shard_map/ppermute | solution.py:236
  125.6 0.1 add.7
  125.6 25.3 %all_to_all.40.landed_ref = f32[8,136,128]{2,1,0:T(8,128)S(1)} all-to-all(f32[8,136,128]{2,1,0:T(8,128)S(1)} %add.7), channel_id=1, replica_groups={{0,256,64,320,128,384,192,448},{32,288,96,352,160,416,224,480},{1,257,6..., dimensions={0} | all-to-all | bytes 1114112 | tf_op jit(solution)/shard_map/all_to_all | solution.py:237
  150.9 0.7 add_landed.1
  151.6 11.9 %all_to_all.41 = f32[16,8,128]{2,1,0:T(8,128)S(1)} all-to-all(f32[16,8,128]{2,1,0:T(8,128)S(1)} %get-tuple-element.17), channel_id=1, replica_groups={{0,1,3,2,8,9,11,10,24,25,27,26,16,17,19,18},{4,5,7,6,12,13,15,14,28,29,..., dimensions={0} | all-to-all | bytes 131072 | tf_op jit(solution)/shard_map/all_to_all | solution.py:201
  163.5 0.6 copy.11
Async XLA Ops:
  0.6 48.2 %copy-start.3 = (s32[1,1,1,16]{3,2,1,0:T(1,128)S(1)}, s32[1,1,1,16]{3,2,1,0:T(1,128)}, u32[]{:S(2)}) copy-start(s32[1,1,1,16]{3,2,1,0:T(1,128)} %param.9) | copy-start | bytes 196
  0.6 48.2 %copy-start = (bf16[1,1,1,16,128,128]{5,4,3,2,1,0:T(8,128)(2,1)S(1)}, bf16[1,1,1,16,128,128]{5,4,3,2,1,0:T(8,128)(2,1)}, u32[]{:S(2)}) copy-start(bf16[1,1,1,16,128,128]{5,4,3,2,1,0:T(8,128)(2,1)} %param.8) | copy-start | bytes 1572868
  37.7 11.1 %collective-permute-start = (f32[8,128,128]{2,1,0:T(8,128)S(1)}, f32[8,128,128]{2,1,0:T(8,128)S(1)}, u32[]{:S(2)}, u32[]{:S(2)}) collective-permute-start(f32[8,128,128]{2,1,0:T(8,128)S(1)} %all_to_all.35.near_ref), channel_id=1, source_target_pairs={{0,32},{4,228},{8,40},{12,236},{16,48},{20,244},{24,56},{28,252},{... | collective-permute-start | bytes 1572872 | tf_op jit(solution)/shard_map/ppermute | solution.py:205
  50.3 4.6 %collective-permute-start.1 = (f32[16,128,128]{2,1,0:T(8,128)S(1)}, f32[16,128,128]{2,1,0:T(8,128)S(1)}, u32[]{:S(2)}, u32[]{:S(2)}) collective-permute-start(f32[16,128,128]{2,1,0:T(8,128)S(1)} %get-tuple-element.12), channel_id=1, source_target_pairs={{0,4},{4,0},{8,12},{12,8},{16,20},{20,16},{24,28},{28,24},{1,5},{5... | collective-permute-start | bytes 3145736 | tf_op jit(solution)/shard_map/ppermute | solution.py:214
  69.7 11.6 %copy-start.1 = (f32[128,128]{1,0:T(8,128)S(1)}, f32[128,128]{1,0:T(8,128)}, u32[]{:S(2)}) copy-start(f32[128,128]{1,0:T(8,128)} %weight_ref.1) | copy-start | bytes 196612
  69.7 11.6 %copy-start.2 = (f32[128,128]{1,0:T(8,128)S(1)}, f32[128,128]{1,0:T(8,128)}, u32[]{:S(2)}) copy-start(f32[128,128]{1,0:T(8,128)} %cot_ref.1) | copy-start | bytes 196612
  106.0 6.7 %collective-permute-start.2 = (f32[4,520,128]{2,1,0:T(8,128)S(1)}, f32[4,520,128]{2,1,0:T(8,128)S(1)}, u32[]{:S(2)}, u32[]{:S(2)}) collective-permute-start(f32[4,520,128]{2,1,0:T(8,128)S(1)} %all_to_all.39.own_ref), channel_id=1, source_target_pairs={{0,4},{4,0},{8,12},{12,8},{16,20},{20,16},{24,28},{28,24},{1,5},{5... | collective-permute-start | bytes 3194888 | tf_op jit(solution)/shard_map/ppermute | solution.py:227
  114.1 11.4 %collective-permute-start.3 = (f32[8,136,128]{2,1,0:T(8,128)S(1)}, f32[8,136,128]{2,1,0:T(8,128)S(1)}, u32[]{:S(2)}, u32[]{:S(2)}) collective-permute-start(f32[8,136,128]{2,1,0:T(8,128)S(1)} %get-tuple-element.16), channel_id=1, source_target_pairs={{0,32},{4,228},{8,40},{12,236},{16,48},{20,244},{24,56},{28,252},{... | collective-permute-start | bytes 1671176 | tf_op jit(solution)/shard_map/ppermute | solution.py:236
